TPU v7x, 512 devices: a whole 4x8x8 slice. The times are simulated.
512 devices in a mesh: ctx: 32 (over y, x), exp: 16 (over z, core).
Axes of the slice: x: 4, y: 8, z: 8, core: 2. Of those that a mesh axis runs over, the one named last changes fastest.
Arguments:
- query_proj: bfloat16 [16384, 2048], P('ctx', 'exp'), may hold values from -6 to 6
- key_proj: bfloat16 [16384, 2048], P('ctx', 'exp'), may hold values from -6 to 6
- value_proj: bfloat16 [16384, 4096], P('ctx', 'exp'), may hold values from -6 to 6
- output_gate: bfloat16 [16384, 4096], P('ctx', 'exp'), may hold values from -6 to 6
- beta_logit: float32 [32, 16384], P('exp', 'ctx'), may hold values from -6 to 6
- log_decay: float32 [32, 16384], P('exp', 'ctx'), may hold values from -3 to 0
- norm_gain: float32 [128], replicated, may hold values from 0.1 to 1.9
- out_weight: bfloat16 [4096, 2048], P('exp'), may hold values from -0.09375 to 0.09375
- residual: bfloat16 [16384, 2048], P(('ctx', 'exp')), may hold values from -6 to 6
- moe_gain: float32 [2048], replicated, may hold values from 0.1 to 1.9
- expert_ids: int32 [16384, 10], P(('ctx', 'exp')), may hold values from 0 to 63, all different within a row; in each aligned block of 32 rows (0 to 31, 32 to 63, ...) at most 6 rows name the same one
- route_weight: float32 [16384, 10], P(('ctx', 'exp')), may hold values from 0.02 to 0.2
- expert_gate: bfloat16 [64, 2048, 512], P('ctx', 'exp'), may hold values from -0.125 to 0.125
- expert_up: bfloat16 [64, 2048, 512], P('ctx', 'exp'), may hold values from -0.125 to 0.125
- expert_down: bfloat16 [64, 512, 2048], P('ctx', None, 'exp'), may hold values from -0.25 to 0.25
Outputs:
- layer_out: bfloat16 [16384, 2048], P(('ctx', 'exp'))
Inputs may be any that keep to these rules, and one draw needn't show every extreme that they name: `expert_ids`: each row names 10 different experts. Among the 32 rows of one device no expert is named by more than 6 rows, and in some devices one expert is named by exactly 6 of them.
All inputs are finite; a program needn't handle non-finite values.
Results may differ from a plain program's by a relative error of at most 0.018.
Values may be sent and summed in bfloat16 or wider, within the bound.
No kernel may reach another device: no remote copies, remote signals or barrier semaphores. Data moves between devices by JAX's collectives and lax.ppermute only.
A program may use at most 64 MiB of HBM per device.

v0:
```python
import jax
import jax.numpy as jnp
from jax import lax
from jax.sharding import PartitionSpec as P

SPAN = 64


largest_score = lax.Precision.HIGHEST


def from_behind(block, axis, distance):
    devices = range(lax.axis_size(axis))
    route = [(i - distance, i) for i in devices if i - distance in devices]
    return lax.ppermute(block, axis, route)


def normalize_rows(values):
    values = values.astype(jnp.float32)
    return values / jnp.sqrt(jnp.sum(values * values, -1, keepdims=True) + 1e-06)


def unit_lower_inverse(lower_part):
    length = lower_part.shape[0]
    identity = jnp.eye(length, dtype=jnp.float32)
    result = identity - lower_part
    power_term = jnp.dot(lower_part, lower_part, precision=largest_score)
    for _ in range((length - 1).bit_length() - 1):
        result = jnp.dot(result, identity + power_term, precision=largest_score)
        power_term = jnp.dot(power_term, power_term, precision=largest_score)
    return result


def span_step(carry_state, pieces):
    queries, key_rows, values, strength, logarithm_count = pieces
    length = queries.shape[0]
    cumulative = jnp.cumsum(logarithm_count)
    gap_logs = cumulative[:, None] - cumulative[None, :]
    row_index = lax.broadcasted_iota(jnp.int32, (length, length), 0)
    col_index = lax.broadcasted_iota(jnp.int32, (length, length), 1)
    within = row_index >= col_index
    decay_mask = jnp.where(within, jnp.exp(jnp.where(within, gap_logs, 0.0)), 0.0)
    strict = jnp.where(row_index > col_index, decay_mask, 0.0)
    lower_part = jnp.dot(key_rows, key_rows.T, precision=largest_score) * strict * strength[None, :]
    start_scale = jnp.exp(cumulative)
    right_side = values - start_scale[:, None] * jnp.dot(
        key_rows, carry_state, precision=largest_score
    )
    update = jnp.dot(unit_lower_inverse(lower_part), right_side, precision=largest_score)
    scores = jnp.dot(queries, key_rows.T, precision=largest_score) * decay_mask * strength[None, :]
    output = start_scale[:, None] * jnp.dot(queries, carry_state, precision=largest_score)
    output = output + jnp.dot(scores, update, precision=largest_score)
    tail_weight = jnp.exp(cumulative[-1] - cumulative) * strength
    carry_state = jnp.exp(cumulative[-1]) * carry_state + jnp.dot(
        (key_rows * tail_weight[:, None]).T, update, precision=largest_score
    )
    return (carry_state, output)


def delta_rule(queries, key_rows, values, strength, logarithm_count, start):
    length = queries.shape[0]
    blocks = length // SPAN
    pieces = (
        queries.reshape(blocks, SPAN, -1),
        key_rows.reshape(blocks, SPAN, -1),
        values.reshape(blocks, SPAN, -1),
        strength.reshape(blocks, SPAN),
        logarithm_count.reshape(blocks, SPAN),
    )
    final, outputs = lax.scan(span_step, start, pieces)
    return (final, outputs.reshape(length, -1))


def shards(
    query_proj,
    key_proj,
    value_proj,
    output_gate,
    beta_logit,
    log_decay,
    norm_gain,
    out_weight,
    residual,
    moe_gain,
    expert_ids,
    route_weight,
    expert_gate,
    expert_up,
    expert_down,
):
    length = query_proj.shape[0]
    head_width = query_proj.shape[1]
    local_heads = beta_logit.shape[0]
    value_dim = value_proj.shape[1] // local_heads
    queries = normalize_rows(query_proj) * head_width ** (-0.5)
    key_rows = normalize_rows(key_proj)
    values = jnp.transpose(
        value_proj.reshape(length, local_heads, value_dim).astype(jnp.float32), (1, 0, 2)
    )
    padded = jnp.concatenate(
        [jnp.zeros((local_heads, length, head_width), jnp.float32), values], -1
    )
    strength = jax.nn.sigmoid(beta_logit)
    identity = jnp.eye(head_width, dtype=jnp.float32)
    start = jnp.concatenate([identity, jnp.zeros((head_width, value_dim), jnp.float32)], 1)
    final, blended_output = jax.vmap(delta_rule, in_axes=(None, None, 0, 0, 0, None))(
        queries, key_rows, padded, strength, log_decay, start
    )
    carried = final[:, :, :head_width]
    offset = final[:, :, head_width:]

    def relay(counter, entry_state):
        leaving = jnp.einsum("hij,hjv->hiv", carried, entry_state, precision=largest_score) + offset
        return from_behind(leaving.astype(jnp.bfloat16), "ctx", 1).astype(leaving.dtype)

    incoming_state = lax.fori_loop(0, lax.axis_size("ctx") - 1, relay, jnp.zeros_like(offset))
    corrected = blended_output[:, :, head_width:] + jnp.einsum(
        "ncb,nbe->nce", blended_output[:, :, :head_width], incoming_state, precision=largest_score
    )
    normed_heads = (
        corrected
        * lax.rsqrt(jnp.mean(corrected * corrected, -1, keepdims=True) + 1e-06)
        * norm_gain
    )
    gates = jnp.transpose(
        output_gate.reshape(length, local_heads, value_dim).astype(jnp.float32), (1, 0, 2)
    )
    gated = (normed_heads * jax.nn.silu(gates)).astype(jnp.bfloat16)
    gated = jnp.transpose(gated, (1, 0, 2)).reshape(length, local_heads * value_dim)
    tokens_here = residual.shape[0]
    attended = lax.psum_scatter(
        jnp.dot(gated, out_weight, preferred_element_type=jnp.float32).astype(jnp.bfloat16),
        "exp",
        scatter_dimension=0,
        tiled=True,
    ).astype(jnp.float32)
    hidden = residual.astype(jnp.float32) + attended
    normed = (
        hidden * lax.rsqrt(jnp.mean(hidden * hidden, -1, keepdims=True) + 1e-06) * moe_gain
    ).astype(jnp.bfloat16)
    width = normed.shape[1]
    experts_here = expert_gate.shape[0]
    groups = lax.axis_size("ctx")
    total_experts = groups * experts_here
    topk = expert_ids.shape[1]
    capacity = min(tokens_here, 6 * tokens_here * topk // (5 * total_experts))
    flat_ids = expert_ids.reshape(-1)
    token_of = jnp.arange(tokens_here * topk, dtype=jnp.int32) // topk
    onehot = (flat_ids[:, None] == jnp.arange(total_experts, dtype=jnp.int32)[None, :]).astype(
        jnp.int32
    )
    earlier_count = jnp.cumsum(onehot, 0) - onehot
    rank = jnp.sum(earlier_count * onehot, 1)
    slot = flat_ids * capacity + rank
    owner = jnp.full((total_experts * capacity,), tokens_here, jnp.int32).at[slot].set(token_of)
    outgoing = jnp.take(normed, owner, axis=0, mode="fill", fill_value=0)
    outgoing = outgoing.reshape(groups, experts_here, capacity, width)
    incoming = lax.all_to_all(outgoing, "ctx", split_axis=0, concat_axis=0, tiled=True)
    answers = []
    for local_expert in range(experts_here):
        rows = incoming[:, local_expert].reshape(groups * capacity, width)
        whole_gate, whole_up, whole_down = (
            lax.all_gather(expert_gate[local_expert], "exp", axis=0, tiled=True),
            lax.all_gather(expert_up[local_expert], "exp", axis=0, tiled=True),
            lax.all_gather(expert_down[local_expert], "exp", axis=1, tiled=True),
        )
        first = jnp.dot(rows, whole_gate, preferred_element_type=jnp.float32)
        second = jnp.dot(rows, whole_up, preferred_element_type=jnp.float32)
        inner = (jax.nn.silu(first) * second).astype(jnp.bfloat16)
        final_result = jnp.dot(inner, whole_down, preferred_element_type=jnp.float32).astype(
            jnp.bfloat16
        )
        answers.append(final_result.reshape(groups, capacity, width))
    returned = lax.all_to_all(jnp.stack(answers, 1), "ctx", split_axis=0, concat_axis=0, tiled=True)
    returned = returned.reshape(total_experts * capacity, width)
    picked = jnp.take(returned, slot, axis=0).reshape(tokens_here, topk, width)
    mixture = jnp.einsum("tk,tkd->td", route_weight, picked.astype(jnp.float32))
    return (hidden + mixture).astype(jnp.bfloat16)


def solution(mesh):
    placed = (
        P("ctx", "exp"),
        P("ctx", "exp"),
        P("ctx", "exp"),
        P("ctx", "exp"),
        P("exp", "ctx"),
        P("exp", "ctx"),
        P(),
        P("exp", None),
        P(("ctx", "exp"), None),
        P(),
        P(("ctx", "exp"), None),
        P(("ctx", "exp"), None),
        P("ctx", "exp", None),
        P("ctx", "exp", None),
        P("ctx", None, "exp"),
    )
    return jax.shard_map(
        shards, mesh=mesh, in_specs=placed, out_specs=P(("ctx", "exp"), None), check_vma=False
    )
```

profile of v0, /device:TPU:4, one launch (start us, length us, event | category | flops | bytes accessed | tf_op | source)
XLA Modules:
  0.0 769.9 jit_solution(18119530776480064976)
XLA Ops:
  11.9 43.9 %while.23 = (s32[]{:T(128)}, f32[2,128,256]{2,1,0:T(8,128)S(1)}, f32[8,2,64,256]{3,2,1,0:T(8,128)}, f32[8,2,64]{2,0,1:T(8,128)S(1)}, f32[8,64,128]{2,1,0:T(8,128...) while((s32[]{:T(128)}, f32[2,128,256]{2,1,0:T(8,128)S(1)}, ...), condition=%wide.region_4.5_spmd, body=%wide.region_2.4_spmd.sunk | while | flops 277315712 | bytes 3520681 | solution.py:70
  57.1 261.1 %while.24 = (s32[]{:T(128)}, f32[2,128,128]{2,1,0:T(8,128)S(1)}, f32[2,128,128]{2,1,0:T(8,128)S(1)}, f32[2,128,128]{2,1,0:T(8,128)S(1)}, s32[]{:T(128)}, /*index=5*/s32[]{:T(128)}) while((s32[]{:T(128)}, f32[2,128,128]{2,1,0:T(8,128)S(1)}, f32[2,128,128]{2,1,0:T(8,128)S(1)}, f32[2,128,128]{2,1,0:T(8,128)S(1)}, s32[]{:T(128)}, ...), condition=%wide.region_6.7_spmd.clone, body=%wide.region_5.6_spmd.clone.sunk | while | flops 50462720 | bytes 917623 | solution.py:116
  57.4 3.1 collective-permute-start
  60.5 3.0 collective-permute-done
  63.9 3.1 collective-permute-start
  67.0 4.8 collective-permute-done
  72.2 2.5 collective-permute-start
  74.7 4.5 collective-permute-done
  79.5 3.8 collective-permute-start
  83.3 2.4 collective-permute-done
  86.0 5.9 collective-permute-start
  94.1 6.4 collective-permute-start
  102.6 6.5 collective-permute-start
  109.1 2.1 collective-permute-done
  111.5 6.3 collective-permute-start
  120.0 6.4 collective-permute-start
  128.6 6.4 collective-permute-start
  137.2 6.4 collective-permute-start
  145.8 6.4 collective-permute-start
  154.4 6.4 collective-permute-start
  163.1 6.6 collective-permute-start
  171.9 6.5 collective-permute-start
  180.6 6.4 collective-permute-start
  189.2 6.4 collective-permute-start
  197.7 6.4 collective-permute-start
  206.3 6.4 collective-permute-start
  214.9 6.4 collective-permute-start
  221.3 2.5 collective-permute-done
  224.1 6.1 collective-permute-start
  232.3 6.5 collective-permute-start
  241.0 6.4 collective-permute-start
  249.6 6.4 collective-permute-start
  258.2 6.4 collective-permute-start
  266.7 6.4 collective-permute-start
  275.3 6.5 collective-permute-start
  284.2 6.3 collective-permute-start
  292.8 6.4 collective-permute-start
  301.3 6.4 collective-permute-start
  309.9 6.4 collective-permute-start
  319.7 2.1 convolution_convert_fusion
  327.9 2.9 scatter_custom_fusion
  331.0 99.3 %reduce-scatter.2.cloned.1.call-done = bf16[32,2048]{1,0:T(8,128)(2,1)} async-done(((bf16[512,2048]{1,0:T(8,128)(2,1)}), bf16[32,2048]{1,0:T(8,128)(2,1)}) %reduce-scatter.2.cloned.1.call-update) | async-done | bytes 131088 | tf_op jit(solution)/shard_map/reduce_scatter | solution.py:131
  432.4 3.1 gather_fusion
  435.6 2.5 gather.13
  438.3 2.8 copy.66
  441.2 9.9 %all-to-all-start = ((bf16[32,2,6,2048]{3,1,2,0:T(2,128)(2,1)}), bf16[32,2,6,2048]{3,1,2,0:T(2,128)(2,1)S(1)}, u32[]{:S(2)}, u32[]{:S(2)}) async-start(bf16[32,2,6,2048]{3,1,2,0:T(2,128)(2,1)} %copy.66), calls=%async_computation.1 | async-start | bytes 3145728 | tf_op jit(solution)/shard_map/all_to_all | solution.py:158
  451.8 35.0 %all-to-all-done = bf16[32,2,6,2048]{3,1,2,0:T(2,128)(2,1)S(1)} async-done(((bf16[32,2,6,2048]{3,1,2,0:T(2,128)(2,1)}), bf16[32,2,6,2048]{3,1,2,0:T(2,128)(2,1)S(1)}, u32[]{:S(2)}, u32[]{:S(2)}) %all-to-all-start) | async-done | bytes 1572896 | tf_op jit(solution)/shard_map/all_to_all | solution.py:158
  486.8 9.4 %slice_reduce_fusion.2 = (bf16[32,6,2048]{2,1,0:T(8,128)(2,1)}, bf16[32,6,2048]{2,1,0:T(8,128)(2,1)}) fusion(bf16[32,2,6,2048]{3,1,2,0:T(2,128)(2,1)S(1)} %all-to-all-done), kind=kLoop, calls=%fused_computation.101 | loop fusion | bytes 3145728 | tf_op jit(solution)/shard_map/slice | solution.py:161
  497.6 2.2 fusion.71
  499.7 17.1 %all-gather.15.cloned.1.call-done = bf16[1,2048,512]{2,1,0:T(8,128)(2,1)} async-done(((bf16[1,128,512]{2,1,0:T(8,128)(2,1)}), bf16[1,2048,512]{2,1,0:T(8,128)(2,1)}) %all-gather.15.cloned.1.call-update) | async-done | bytes 2097168 | tf_op jit(solution)/shard_map/all_gather | solution.py:164
  516.8 44.3 %all-gather.17.cloned.1.call-done = bf16[1,512,2048]{2,1,0:T(8,128)(2,1)} async-done(((bf16[1,512,128]{2,1,0:T(8,128)(2,1)}), bf16[1,512,2048]{2,1,0:T(8,128)(2,1)}) %all-gather.17.cloned.1.call-update) | async-done | bytes 2097168 | tf_op jit(solution)/shard_map/all_gather | solution.py:165
  561.1 4.2 convolution_convert_fusion.2
  568.0 37.0 %all-gather.19.cloned.1.call-done = bf16[1,2048,512]{2,1,0:T(8,128)(2,1)} async-done(((bf16[1,128,512]{2,1,0:T(8,128)(2,1)}), bf16[1,2048,512]{2,1,0:T(8,128)(2,1)}) %all-gather.19.cloned.1.call-update) | async-done | bytes 2097168 | tf_op jit(solution)/shard_map/all_gather | solution.py:163
  605.0 3.2 fusion.66
  608.2 40.1 %all-gather.21.cloned.1.call-done = bf16[1,2048,512]{2,1,0:T(8,128)(2,1)} async-done(((bf16[1,128,512]{2,1,0:T(8,128)(2,1)}), bf16[1,2048,512]{2,1,0:T(8,128)(2,1)}) %all-gather.21.cloned.1.call-update) | async-done | bytes 2097168 | tf_op jit(solution)/shard_map/all_gather | solution.py:164
  648.3 44.4 %all-gather.23.cloned.1.call-done = bf16[1,512,2048]{2,1,0:T(8,128)(2,1)} async-done(((bf16[1,512,128]{2,1,0:T(8,128)(2,1)}), bf16[1,512,2048]{2,1,0:T(8,128)(2,1)}) %all-gather.23.cloned.1.call-update) | async-done | bytes 2097168 | tf_op jit(solution)/shard_map/all_gather | solution.py:165
  692.7 4.3 convolution_convert_fusion.1
  698.9 2.8 copy.67
  701.7 10.0 %all-to-all-start.1 = ((bf16[32,2,6,2048]{3,1,2,0:T(2,128)(2,1)}), bf16[32,2,6,2048]{3,1,2,0:T(2,128)(2,1)S(1)}, u32[]{:S(2)}, u32[]{:S(2)}) async-start(bf16[32,2,6,2048]{3,1,2,0:T(2,128)(2,1)} %copy.67), calls=%async_computation.2 | async-start | bytes 3145728 | tf_op jit(solution)/shard_map/all_to_all | solution.py:174
  711.9 39.5 %all-to-all-done.1 = bf16[32,2,6,2048]{3,1,2,0:T(2,128)(2,1)S(1)} async-done(((bf16[32,2,6,2048]{3,1,2,0:T(2,128)(2,1)}), bf16[32,2,6,2048]{3,1,2,0:T(2,128)(2,1)S(1)}, u32[]{:S(2)}, u32[]{:S(2)}) %all-to-all-start.1) | async-done | bytes 1572896 | tf_op jit(solution)/shard_map/all_to_all | solution.py:174
  751.4 2.1 copy.68
  753.5 2.6 reshape.187
  756.1 3.0 gather_fusion.1
  759.1 2.3 gather.15
  (392 shorter events, 123.6 us)
Async XLA Ops:
  6.5 313.1 %copy-start = (bf16[256,2048]{1,0:T(8,128)(2,1)S(1)}, bf16[256,2048]{1,0:T(8,128)(2,1)}, u32[]{:S(2)}) copy-start(bf16[256,2048]{1,0:T(8,128)(2,1)} %param.26) | copy-start | bytes 3145732
  6.5 423.8 %reduce-scatter.2.cloned.1.call-start = ((), (), s32[]{:S(2)}) async-start(), calls=%async_computation.3 | async-start | bytes 2228224 | tf_op jit(solution)/shard_map/reduce_scatter | solution.py:131
  7.9 0.9 copy-start.5
  7.9 2.3 copy-start.6
  57.1 261.9 %copy-start.7 = (bf16[512,256]{1,0:T(8,128)(2,1)S(1)}, bf16[512,256]{1,0:T(8,128)(2,1)}, u32[]{:S(2)}) copy-start(bf16[512,256]{1,0:T(8,128)(2,1)} %param.22) | copy-start | bytes 786436
  57.4 6.2 collective-permute-start
  63.9 8.0 %collective-permute-start = (bf16[2,128,128]{2,1,0:T(8,128)(2,1)S(1)}, bf16[2,128,128]{2,1,0:T(8,128)(2,1)S(1)}, u32[]{:S(2)}, u32[]{:S(2)}) collective-permute-start(bf16[2,128,128]{2,1,0:T(8,128)(2,1)S(1)} %fusion.269), channel_id=1, source_target_pairs={{0,16},{16,32},{32,48},{48,64},{64,80},{80,96},{96,112},{112,128},... | collective-permute-start | bytes 196616 | tf_op jit(solution)/shard_map/while/body/eval_jaxpr/ppermute | solution.py:15
  72.2 7.0 collective-permute-start
  79.5 6.2 collective-permute-start
  86.0 7.8 %collective-permute-start = (bf16[2,128,128]{2,1,0:T(8,128)(2,1)S(1)}, bf16[2,128,128]{2,1,0:T(8,128)(2,1)S(1)}, u32[]{:S(2)}, u32[]{:S(2)}) collective-permute-start(bf16[2,128,128]{2,1,0:T(8,128)(2,1)S(1)} %fusion.269), channel_id=1, source_target_pairs={{0,16},{16,32},{32,48},{48,64},{64,80},{80,96},{96,112},{112,128},... | collective-permute-start | bytes 196616 | tf_op jit(solution)/shard_map/while/body/eval_jaxpr/ppermute | solution.py:15
  94.1 8.3 %collective-permute-start = (bf16[2,128,128]{2,1,0:T(8,128)(2,1)S(1)}, bf16[2,128,128]{2,1,0:T(8,128)(2,1)S(1)}, u32[]{:S(2)}, u32[]{:S(2)}) collective-permute-start(bf16[2,128,128]{2,1,0:T(8,128)(2,1)S(1)} %fusion.269), channel_id=1, source_target_pairs={{0,16},{16,32},{32,48},{48,64},{64,80},{80,96},{96,112},{112,128},... | collective-permute-start | bytes 196616 | tf_op jit(solution)/shard_map/while/body/eval_jaxpr/ppermute | solution.py:15
  102.6 8.6 %collective-permute-start = (bf16[2,128,128]{2,1,0:T(8,128)(2,1)S(1)}, bf16[2,128,128]{2,1,0:T(8,128)(2,1)S(1)}, u32[]{:S(2)}, u32[]{:S(2)}) collective-permute-start(bf16[2,128,128]{2,1,0:T(8,128)(2,1)S(1)} %fusion.269), channel_id=1, source_target_pairs={{0,16},{16,32},{32,48},{48,64},{64,80},{80,96},{96,112},{112,128},... | collective-permute-start | bytes 196616 | tf_op jit(solution)/shard_map/while/body/eval_jaxpr/ppermute | solution.py:15
  111.5 8.2 %collective-permute-start = (bf16[2,128,128]{2,1,0:T(8,128)(2,1)S(1)}, bf16[2,128,128]{2,1,0:T(8,128)(2,1)S(1)}, u32[]{:S(2)}, u32[]{:S(2)}) collective-permute-start(bf16[2,128,128]{2,1,0:T(8,128)(2,1)S(1)} %fusion.269), channel_id=1, source_target_pairs={{0,16},{16,32},{32,48},{48,64},{64,80},{80,96},{96,112},{112,128},... | collective-permute-start | bytes 196616 | tf_op jit(solution)/shard_map/while/body/eval_jaxpr/ppermute | solution.py:15
  120.0 8.3 %collective-permute-start = (bf16[2,128,128]{2,1,0:T(8,128)(2,1)S(1)}, bf16[2,128,128]{2,1,0:T(8,128)(2,1)S(1)}, u32[]{:S(2)}, u32[]{:S(2)}) collective-permute-start(bf16[2,128,128]{2,1,0:T(8,128)(2,1)S(1)} %fusion.269), channel_id=1, source_target_pairs={{0,16},{16,32},{32,48},{48,64},{64,80},{80,96},{96,112},{112,128},... | collective-permute-start | bytes 196616 | tf_op jit(solution)/shard_map/while/body/eval_jaxpr/ppermute | solution.py:15
  128.6 8.3 %collective-permute-start = (bf16[2,128,128]{2,1,0:T(8,128)(2,1)S(1)}, bf16[2,128,128]{2,1,0:T(8,128)(2,1)S(1)}, u32[]{:S(2)}, u32[]{:S(2)}) collective-permute-start(bf16[2,128,128]{2,1,0:T(8,128)(2,1)S(1)} %fusion.269), channel_id=1, source_target_pairs={{0,16},{16,32},{32,48},{48,64},{64,80},{80,96},{96,112},{112,128},... | collective-permute-start | bytes 196616 | tf_op jit(solution)/shard_map/while/body/eval_jaxpr/ppermute | solution.py:15
  137.2 8.3 %collective-permute-start = (bf16[2,128,128]{2,1,0:T(8,128)(2,1)S(1)}, bf16[2,128,128]{2,1,0:T(8,128)(2,1)S(1)}, u32[]{:S(2)}, u32[]{:S(2)}) collective-permute-start(bf16[2,128,128]{2,1,0:T(8,128)(2,1)S(1)} %fusion.269), channel_id=1, source_target_pairs={{0,16},{16,32},{32,48},{48,64},{64,80},{80,96},{96,112},{112,128},... | collective-permute-start | bytes 196616 | tf_op jit(solution)/shard_map/while/body/eval_jaxpr/ppermute | solution.py:15
  145.8 8.3 %collective-permute-start = (bf16[2,128,128]{2,1,0:T(8,128)(2,1)S(1)}, bf16[2,128,128]{2,1,0:T(8,128)(2,1)S(1)}, u32[]{:S(2)}, u32[]{:S(2)}) collective-permute-start(bf16[2,128,128]{2,1,0:T(8,128)(2,1)S(1)} %fusion.269), channel_id=1, source_target_pairs={{0,16},{16,32},{32,48},{48,64},{64,80},{80,96},{96,112},{112,128},... | collective-permute-start | bytes 196616 | tf_op jit(solution)/shard_map/while/body/eval_jaxpr/ppermute | solution.py:15
  154.4 8.4 %collective-permute-start = (bf16[2,128,128]{2,1,0:T(8,128)(2,1)S(1)}, bf16[2,128,128]{2,1,0:T(8,128)(2,1)S(1)}, u32[]{:S(2)}, u32[]{:S(2)}) collective-permute-start(bf16[2,128,128]{2,1,0:T(8,128)(2,1)S(1)} %fusion.269), channel_id=1, source_target_pairs={{0,16},{16,32},{32,48},{48,64},{64,80},{80,96},{96,112},{112,128},... | collective-permute-start | bytes 196616 | tf_op jit(solution)/shard_map/while/body/eval_jaxpr/ppermute | solution.py:15
  163.1 8.5 %collective-permute-start = (bf16[2,128,128]{2,1,0:T(8,128)(2,1)S(1)}, bf16[2,128,128]{2,1,0:T(8,128)(2,1)S(1)}, u32[]{:S(2)}, u32[]{:S(2)}) collective-permute-start(bf16[2,128,128]{2,1,0:T(8,128)(2,1)S(1)} %fusion.269), channel_id=1, source_target_pairs={{0,16},{16,32},{32,48},{48,64},{64,80},{80,96},{96,112},{112,128},... | collective-permute-start | bytes 196616 | tf_op jit(solution)/shard_map/while/body/eval_jaxpr/ppermute | solution.py:15
  171.9 8.4 %collective-permute-start = (bf16[2,128,128]{2,1,0:T(8,128)(2,1)S(1)}, bf16[2,128,128]{2,1,0:T(8,128)(2,1)S(1)}, u32[]{:S(2)}, u32[]{:S(2)}) collective-permute-start(bf16[2,128,128]{2,1,0:T(8,128)(2,1)S(1)} %fusion.269), channel_id=1, source_target_pairs={{0,16},{16,32},{32,48},{48,64},{64,80},{80,96},{96,112},{112,128},... | collective-permute-start | bytes 196616 | tf_op jit(solution)/shard_map/while/body/eval_jaxpr/ppermute | solution.py:15
  180.6 8.3 %collective-permute-start = (bf16[2,128,128]{2,1,0:T(8,128)(2,1)S(1)}, bf16[2,128,128]{2,1,0:T(8,128)(2,1)S(1)}, u32[]{:S(2)}, u32[]{:S(2)}) collective-permute-start(bf16[2,128,128]{2,1,0:T(8,128)(2,1)S(1)} %fusion.269), channel_id=1, source_target_pairs={{0,16},{16,32},{32,48},{48,64},{64,80},{80,96},{96,112},{112,128},... | collective-permute-start | bytes 196616 | tf_op jit(solution)/shard_map/while/body/eval_jaxpr/ppermute | solution.py:15
  189.2 8.3 %collective-permute-start = (bf16[2,128,128]{2,1,0:T(8,128)(2,1)S(1)}, bf16[2,128,128]{2,1,0:T(8,128)(2,1)S(1)}, u32[]{:S(2)}, u32[]{:S(2)}) collective-permute-start(bf16[2,128,128]{2,1,0:T(8,128)(2,1)S(1)} %fusion.269), channel_id=1, source_target_pairs={{0,16},{16,32},{32,48},{48,64},{64,80},{80,96},{96,112},{112,128},... | collective-permute-start | bytes 196616 | tf_op jit(solution)/shard_map/while/body/eval_jaxpr/ppermute | solution.py:15
  197.7 8.3 %collective-permute-start = (bf16[2,128,128]{2,1,0:T(8,128)(2,1)S(1)}, bf16[2,128,128]{2,1,0:T(8,128)(2,1)S(1)}, u32[]{:S(2)}, u32[]{:S(2)}) collective-permute-start(bf16[2,128,128]{2,1,0:T(8,128)(2,1)S(1)} %fusion.269), channel_id=1, source_target_pairs={{0,16},{16,32},{32,48},{48,64},{64,80},{80,96},{96,112},{112,128},... | collective-permute-start | bytes 196616 | tf_op jit(solution)/shard_map/while/body/eval_jaxpr/ppermute | solution.py:15
  206.3 8.3 %collective-permute-start = (bf16[2,128,128]{2,1,0:T(8,128)(2,1)S(1)}, bf16[2,128,128]{2,1,0:T(8,128)(2,1)S(1)}, u32[]{:S(2)}, u32[]{:S(2)}) collective-permute-start(bf16[2,128,128]{2,1,0:T(8,128)(2,1)S(1)} %fusion.269), channel_id=1, source_target_pairs={{0,16},{16,32},{32,48},{48,64},{64,80},{80,96},{96,112},{112,128},... | collective-permute-start | bytes 196616 | tf_op jit(solution)/shard_map/while/body/eval_jaxpr/ppermute | solution.py:15
  214.9 8.8 %collective-permute-start = (bf16[2,128,128]{2,1,0:T(8,128)(2,1)S(1)}, bf16[2,128,128]{2,1,0:T(8,128)(2,1)S(1)}, u32[]{:S(2)}, u32[]{:S(2)}) collective-permute-start(bf16[2,128,128]{2,1,0:T(8,128)(2,1)S(1)} %fusion.269), channel_id=1, source_target_pairs={{0,16},{16,32},{32,48},{48,64},{64,80},{80,96},{96,112},{112,128},... | collective-permute-start | bytes 196616 | tf_op jit(solution)/shard_map/while/body/eval_jaxpr/ppermute | solution.py:15
  224.1 8.0 %collective-permute-start = (bf16[2,128,128]{2,1,0:T(8,128)(2,1)S(1)}, bf16[2,128,128]{2,1,0:T(8,128)(2,1)S(1)}, u32[]{:S(2)}, u32[]{:S(2)}) collective-permute-start(bf16[2,128,128]{2,1,0:T(8,128)(2,1)S(1)} %fusion.269), channel_id=1, source_target_pairs={{0,16},{16,32},{32,48},{48,64},{64,80},{80,96},{96,112},{112,128},... | collective-permute-start | bytes 196616 | tf_op jit(solution)/shard_map/while/body/eval_jaxpr/ppermute | solution.py:15
  232.3 8.4 %collective-permute-start = (bf16[2,128,128]{2,1,0:T(8,128)(2,1)S(1)}, bf16[2,128,128]{2,1,0:T(8,128)(2,1)S(1)}, u32[]{:S(2)}, u32[]{:S(2)}) collective-permute-start(bf16[2,128,128]{2,1,0:T(8,128)(2,1)S(1)} %fusion.269), channel_id=1, source_target_pairs={{0,16},{16,32},{32,48},{48,64},{64,80},{80,96},{96,112},{112,128},... | collective-permute-start | bytes 196616 | tf_op jit(solution)/shard_map/while/body/eval_jaxpr/ppermute | solution.py:15
  241.0 8.3 %collective-permute-start = (bf16[2,128,128]{2,1,0:T(8,128)(2,1)S(1)}, bf16[2,128,128]{2,1,0:T(8,128)(2,1)S(1)}, u32[]{:S(2)}, u32[]{:S(2)}) collective-permute-start(bf16[2,128,128]{2,1,0:T(8,128)(2,1)S(1)} %fusion.269), channel_id=1, source_target_pairs={{0,16},{16,32},{32,48},{48,64},{64,80},{80,96},{96,112},{112,128},... | collective-permute-start | bytes 196616 | tf_op jit(solution)/shard_map/while/body/eval_jaxpr/ppermute | solution.py:15
  249.6 8.3 %collective-permute-start = (bf16[2,128,128]{2,1,0:T(8,128)(2,1)S(1)}, bf16[2,128,128]{2,1,0:T(8,128)(2,1)S(1)}, u32[]{:S(2)}, u32[]{:S(2)}) collective-permute-start(bf16[2,128,128]{2,1,0:T(8,128)(2,1)S(1)} %fusion.269), channel_id=1, source_target_pairs={{0,16},{16,32},{32,48},{48,64},{64,80},{80,96},{96,112},{112,128},... | collective-permute-start | bytes 196616 | tf_op jit(solution)/shard_map/while/body/eval_jaxpr/ppermute | solution.py:15
  258.2 8.3 %collective-permute-start = (bf16[2,128,128]{2,1,0:T(8,128)(2,1)S(1)}, bf16[2,128,128]{2,1,0:T(8,128)(2,1)S(1)}, u32[]{:S(2)}, u32[]{:S(2)}) collective-permute-start(bf16[2,128,128]{2,1,0:T(8,128)(2,1)S(1)} %fusion.269), channel_id=1, source_target_pairs={{0,16},{16,32},{32,48},{48,64},{64,80},{80,96},{96,112},{112,128},... | collective-permute-start | bytes 196616 | tf_op jit(solution)/shard_map/while/body/eval_jaxpr/ppermute | solution.py:15
  266.7 8.3 %collective-permute-start = (bf16[2,128,128]{2,1,0:T(8,128)(2,1)S(1)}, bf16[2,128,128]{2,1,0:T(8,128)(2,1)S(1)}, u32[]{:S(2)}, u32[]{:S(2)}) collective-permute-start(bf16[2,128,128]{2,1,0:T(8,128)(2,1)S(1)} %fusion.269), channel_id=1, source_target_pairs={{0,16},{16,32},{32,48},{48,64},{64,80},{80,96},{96,112},{112,128},... | collective-permute-start | bytes 196616 | tf_op jit(solution)/shard_map/while/body/eval_jaxpr/ppermute | solution.py:15
  275.3 8.6 %collective-permute-start = (bf16[2,128,128]{2,1,0:T(8,128)(2,1)S(1)}, bf16[2,128,128]{2,1,0:T(8,128)(2,1)S(1)}, u32[]{:S(2)}, u32[]{:S(2)}) collective-permute-start(bf16[2,128,128]{2,1,0:T(8,128)(2,1)S(1)} %fusion.269), channel_id=1, source_target_pairs={{0,16},{16,32},{32,48},{48,64},{64,80},{80,96},{96,112},{112,128},... | collective-permute-start | bytes 196616 | tf_op jit(solution)/shard_map/while/body/eval_jaxpr/ppermute | solution.py:15
  284.2 8.2 %collective-permute-start = (bf16[2,128,128]{2,1,0:T(8,128)(2,1)S(1)}, bf16[2,128,128]{2,1,0:T(8,128)(2,1)S(1)}, u32[]{:S(2)}, u32[]{:S(2)}) collective-permute-start(bf16[2,128,128]{2,1,0:T(8,128)(2,1)S(1)} %fusion.269), channel_id=1, source_target_pairs={{0,16},{16,32},{32,48},{48,64},{64,80},{80,96},{96,112},{112,128},... | collective-permute-start | bytes 196616 | tf_op jit(solution)/shard_map/while/body/eval_jaxpr/ppermute | solution.py:15
  292.8 8.3 %collective-permute-start = (bf16[2,128,128]{2,1,0:T(8,128)(2,1)S(1)}, bf16[2,128,128]{2,1,0:T(8,128)(2,1)S(1)}, u32[]{:S(2)}, u32[]{:S(2)}) collective-permute-start(bf16[2,128,128]{2,1,0:T(8,128)(2,1)S(1)} %fusion.269), channel_id=1, source_target_pairs={{0,16},{16,32},{32,48},{48,64},{64,80},{80,96},{96,112},{112,128},... | collective-permute-start | bytes 196616 | tf_op jit(solution)/shard_map/while/body/eval_jaxpr/ppermute | solution.py:15
  301.3 8.3 %collective-permute-start = (bf16[2,128,128]{2,1,0:T(8,128)(2,1)S(1)}, bf16[2,128,128]{2,1,0:T(8,128)(2,1)S(1)}, u32[]{:S(2)}, u32[]{:S(2)}) collective-permute-start(bf16[2,128,128]{2,1,0:T(8,128)(2,1)S(1)} %fusion.269), channel_id=1, source_target_pairs={{0,16},{16,32},{32,48},{48,64},{64,80},{80,96},{96,112},{112,128},... | collective-permute-start | bytes 196616 | tf_op jit(solution)/shard_map/while/body/eval_jaxpr/ppermute | solution.py:15
  309.9 8.3 %collective-permute-start = (bf16[2,128,128]{2,1,0:T(8,128)(2,1)S(1)}, bf16[2,128,128]{2,1,0:T(8,128)(2,1)S(1)}, u32[]{:S(2)}, u32[]{:S(2)}) collective-permute-start(bf16[2,128,128]{2,1,0:T(8,128)(2,1)S(1)} %fusion.269), channel_id=1, source_target_pairs={{0,16},{16,32},{32,48},{48,64},{64,80},{80,96},{96,112},{112,128},... | collective-permute-start | bytes 196616 | tf_op jit(solution)/shard_map/while/body/eval_jaxpr/ppermute | solution.py:15
  318.2 1.1 copy-start.14
  321.7 0.9 copy-start.8
  321.7 1.7 copy-start.9
  321.7 2.6 copy-start.10
  321.7 4.5 copy-start.11
  321.7 108.6 %copy-start.3 = (bf16[32,2048]{1,0:T(8,128)(2,1)S(1)}, bf16[32,2048]{1,0:T(8,128)(2,1)}, u32[]{:S(2)}) copy-start(bf16[32,2048]{1,0:T(8,128)(2,1)} %param.27) | copy-start | bytes 393220
  321.8 109.7 %copy-start.12 = (f32[2048]{0:T(1024)S(1)}, f32[2048]{0:T(1024)}, u32[]{:S(2)}) copy-start(f32[2048]{0:T(1024)} %param.28) | copy-start | bytes 24580
  321.8 175.8 %all-gather.13.cloned.1.call-start = ((), (), s32[]{:S(2)}) async-start(), calls=%async_computation.4 | async-start | bytes 2228224 | tf_op jit(solution)/shard_map/all_gather | solution.py:163
  323.4 193.4 %all-gather.15.cloned.1.call-start = ((), (), s32[]{:S(2)}) async-start(), calls=%async_computation.5 | async-start | bytes 2228224 | tf_op jit(solution)/shard_map/all_gather | solution.py:164
  324.2 236.9 %all-gather.17.cloned.1.call-start = ((), (), s32[]{:S(2)}) async-start(), calls=%async_computation.6 | async-start | bytes 2228224 | tf_op jit(solution)/shard_map/all_gather | solution.py:165
  325.0 279.9 %all-gather.19.cloned.1.call-start = ((), (), s32[]{:S(2)}) async-start(), calls=%async_computation.7 | async-start | bytes 2228224 | tf_op jit(solution)/shard_map/all_gather | solution.py:163
  325.6 322.6 %all-gather.21.cloned.1.call-start = ((), (), s32[]{:S(2)}) async-start(), calls=%async_computation.8 | async-start | bytes 2228224 | tf_op jit(solution)/shard_map/all_gather | solution.py:164
  441.2 45.6 %all-to-all-start = ((bf16[32,2,6,2048]{3,1,2,0:T(2,128)(2,1)}), bf16[32,2,6,2048]{3,1,2,0:T(2,128)(2,1)S(1)}, u32[]{:S(2)}, u32[]{:S(2)}) async-start(bf16[32,2,6,2048]{3,1,2,0:T(2,128)(2,1)} %copy.66), calls=%async_computation.1 | async-start | bytes 3145728 | tf_op jit(solution)/shard_map/all_to_all | solution.py:158
  451.0 241.7 %all-gather.23.cloned.1.call-start = ((), (), s32[]{:S(2)}) async-start(), calls=%async_computation.9 | async-start | bytes 2228224 | tf_op jit(solution)/shard_map/all_gather | solution.py:165
  565.3 1.5 copy-start.1
  568.0 124.8 %copy-start.2 = (bf16[192,2048]{1,0:T(8,128)(2,1)S(1)}, bf16[192,2048]{1,0:T(8,128)(2,1)}, u32[]{:S(2)}) copy-start(bf16[192,2048]{1,0:T(8,128)(2,1)} %reshape_squeeze.7) | copy-start | bytes 2359300
  701.7 10.1 %copy-start.13 = (f32[32,10]{0,1:T(8,128)S(1)}, f32[32,10]{0,1:T(8,128)}, u32[]{:S(2)}) copy-start(f32[32,10]{0,1:T(8,128)} %param.30) | copy-start | bytes 3844
  701.7 49.7 %all-to-all-start.1 = ((bf16[32,2,6,2048]{3,1,2,0:T(2,128)(2,1)}), bf16[32,2,6,2048]{3,1,2,0:T(2,128)(2,1)S(1)}, u32[]{:S(2)}, u32[]{:S(2)}) async-start(bf16[32,2,6,2048]{3,1,2,0:T(2,128)(2,1)} %copy.67), calls=%async_computation.2 | async-start | bytes 3145728 | tf_op jit(solution)/shard_map/all_to_all | solution.py:174
  761.4 0.9 copy-start.4
Sparse Core Ops, SparseCore 0:
  321.9 108.4 reduce-scatter.1
  432.5 40.8 all-gather.12
  475.5 41.2 all-gather.14
  518.7 42.3 all-gather.16
  563.1 41.8 all-gather.18
  607.0 41.2 all-gather.20
  650.3 42.3 all-gather.22
where the time goes:
time: 772 us; the launch traced here: 770 us
  waiting for transfers between devices  425 us (55%)
  starting transfers between devices  205 us (27%)
  matrix products  63.9 us (8%)
  local copies, waits for them, and re-layouts  49.5 us (6%)
  between operations  14 us (2%)
  other arithmetic  10.3 us (1%)
    ppermute x31, starting transfers between devices, from_behind(): return lax.ppermute(block, axis, route)  185 us
    reduce_scatter x1, waiting for transfers between devices, shards(): lax.psum_scatter(jnp.dot(gated, out_weight, preferred_element_type=jnp.fl...  99.3 us
    all_gather x2, waiting for transfers between devices, shards(): lax.all_gather(expert_down[local_expert], 'exp', axis=1, tiled=True)  88.7 us
    ppermute x31, waiting for transfers between devices, from_behind(): return lax.ppermute(block, axis, route)  66.7 us
    all_gather x2, waiting for transfers between devices, shards(): lax.all_gather(expert_up[local_expert], 'exp', axis=0, tiled=True)  57.2 us
    all_to_all x1, waiting for transfers between devices, shards(): lax.all_to_all(jnp.stack(answers, 1), 'ctx', split_axis=0, concat_axis=0,...  39.5 us
    all_gather x2, waiting for transfers between devices, shards(): lax.all_gather(expert_gate[local_expert], 'exp', axis=0, tiled=True)  37 us
    all_to_all x1, waiting for transfers between devices, shards(): lax.all_to_all(outgoing, 'ctx', split_axis=0, concat_axis=0, tiled=True)  35 us
  transfers between devices with their start and end apart: 40, of which 39 were waited for; matrix products, arithmetic and copies ran while one was open for 5% of the time, Pallas kernels for 0%

commit v1 on v0

v1 whole, which is shorter than its diff:
```python
import functools

import jax
import jax.numpy as jnp
from jax import lax
from jax.experimental import pallas as pl
from jax.experimental.pallas import tpu as pltpu
from jax.sharding import PartitionSpec as P

BLOCK = 128
f32 = jnp.float32
bf16 = jnp.bfloat16
VMEM = pltpu.VMEM
SMEM = pltpu.SMEM
MIB = 1 << 20


def vmem():
    return pl.BlockSpec(memory_space=VMEM)


def smem():
    return pl.BlockSpec(memory_space=SMEM)


def params(mib):
    return pltpu.CompilerParams(vmem_limit_bytes=mib * MIB)


def cost(flops, moved):
    return pl.CostEstimate(flops=int(flops), bytes_accessed=int(moved), transcendentals=0)


def mm(left, right):
    return jnp.dot(left.astype(bf16), right.astype(bf16), preferred_element_type=f32)


def mm_nt(left, right):
    return lax.dot_general(
        left.astype(bf16),
        right.astype(bf16),
        (((1,), (1,)), ((), ())),
        preferred_element_type=f32,
    )


def sigmoid(value):
    return 1.0 / (1.0 + jnp.exp(-value))


def scan_kernel(heads, q_ref, k_ref, v_ref, beta_ref, log_ref, carry_ref, blend_ref, own_ref):
    length, dk = q_ref.shape
    count = length // BLOCK
    row = lax.broadcasted_iota(jnp.int32, (BLOCK, BLOCK), 0)
    col = lax.broadcasted_iota(jnp.int32, (BLOCK, BLOCK), 1)
    problems = []
    for c in range(count):
        span = slice(c * BLOCK, (c + 1) * BLOCK)
        keys, queries = k_ref[span, :], q_ref[span, :]
        key_values, query_values = keys.astype(f32), queries.astype(f32)
        key_scale = lax.rsqrt(jnp.sum(key_values * key_values, 1, keepdims=True) + 1e-06)
        query_scale = lax.rsqrt(
            jnp.sum(query_values * query_values, 1, keepdims=True) + 1e-06
        ) * dk ** (-0.5)
        key_scale_row = jnp.sum(jnp.where(row == col, key_scale, 0.0), 0, keepdims=True)
        key_key = mm_nt(keys, keys) * key_scale * key_scale_row
        query_key = mm_nt(queries, keys) * query_scale * key_scale_row
        keys_t = jnp.transpose(key_values)
        for h in range(heads):
            logs = log_ref[h : h + 1, span]
            beta = sigmoid(beta_ref[h : h + 1, span])
            logs_col = jnp.sum(jnp.where(row == col, logs, 0.0), 1, keepdims=True)
            total_row = jnp.sum(jnp.where(row <= col, logs_col, 0.0), 0, keepdims=True)
            total_col = jnp.sum(jnp.where(col <= row, logs, 0.0), 1, keepdims=True)
            within = row >= col
            mask = jnp.where(
                within, jnp.exp(jnp.where(within, total_col - total_row, 0.0)), 0.0
            ) * beta
            lower = jnp.where(row > col, key_key * mask, 0.0)
            end = total_row[:, BLOCK - 1 : BLOCK]
            problems.append(
                dict(
                    lower=lower,
                    inverse=jnp.where(row == col, 1.0, 0.0)
                    - jnp.where(row // 2 == col // 2, lower, 0.0),
                    scores=(query_key * mask).astype(bf16),
                    into=jnp.exp(total_row) * key_scale_row,
                    queries=query_values * (jnp.exp(total_col) * query_scale),
                    tail=(keys_t * (jnp.exp(end - total_row) * beta * key_scale_row)).astype(bf16),
                    gain=jnp.exp(end),
                    keys=keys,
                    values=v_ref[span, h * dk : (h + 1) * dk],
                )
            )
    width = 2
    while width < BLOCK:
        pick = (row // (2 * width) == col // (2 * width)) & (row // width != col // width)
        for p in problems:
            inverse = p["inverse"].astype(bf16)
            step = mm(inverse, jnp.where(pick, p["lower"], 0.0))
            p["inverse"] = p["inverse"] - mm(step, inverse)
        width *= 2
    for p in problems:
        p["both"] = jnp.concatenate(
            [mm(p["inverse"] * p["into"], p["keys"]), mm(p["inverse"], p["values"])], 1
        ).astype(bf16)
    for p in problems:
        p["seen"] = mm(p["scores"], p["both"])
        p["push"] = mm(p["tail"], p["both"])
    states = []
    for h in range(heads):
        states.append(
            jnp.concatenate(
                [jnp.where(row == col, 1.0, 0.0), jnp.zeros((dk, dk), f32)], 1
            )
        )
    for c in range(count):
        span = slice(c * BLOCK, (c + 1) * BLOCK)
        for h in range(heads):
            p = problems[c * heads + h]
            state = states[h]
            low = state.astype(bf16)
            out = mm(p["queries"] - p["seen"][:, :dk], low)
            blend_ref[h, span, :] = out[:, :dk].astype(bf16)
            own_ref[h, span, :] = out[:, dk:] + p["seen"][:, dk:]
            push = p["push"]
            moved = mm(push[:, :dk], low)
            states[h] = jnp.concatenate(
                [
                    p["gain"] * state[:, :dk] - moved[:, :dk],
                    p["gain"] * state[:, dk:] - moved[:, dk:] + push[:, dk:],
                ],
                1,
            )
    for h in range(heads):
        carry_ref[h, :dk, :] = jnp.transpose(states[h][:, :dk]).astype(bf16)
        carry_ref[h, dk:, :] = jnp.transpose(states[h][:, dk:]).astype(bf16)


def follow(late, early):
    dk = late.shape[-1]
    moved = mm(early, late[:dk])
    return jnp.concatenate([moved[:dk], moved[dk:] + late[dk:].astype(f32)], 0).astype(bf16)


def row_kernel(where_ref, m0, m1, m2, m3, total_ref, before_ref):
    x = where_ref[0]
    maps = (m0, m1, m2, m3)
    heads, _, dk = m0.shape
    half = dk * heads // 4
    for place in range(4):

        @pl.when(x == place)
        def _():
            ordered = [maps[(place - j) % 4] for j in range(4)]
            for h in range(heads):
                parts = [ordered[j][h] for j in range(4)]
                prefix = parts[0]
                for j in range(1, place):
                    prefix = follow(parts[j], prefix)
                if place == 0:
                    eye = lax.broadcasted_iota(jnp.int32, (dk, dk), 0) == (
                        lax.broadcasted_iota(jnp.int32, (dk, dk), 1)
                    )
                    prefix = jnp.concatenate(
                        [jnp.where(eye, 1.0, 0.0), jnp.zeros((dk, dk), f32)], 0
                    ).astype(bf16)
                before_ref[h] = prefix
                if h == place // 2:
                    low = dk + (place % 2) * half
                    cut = [
                        jnp.concatenate([part[:dk], part[low : low + half]], 0) for part in parts
                    ]
                    total = cut[0]
                    for j in range(1, 4):
                        total = follow(cut[j], total)
                    total_ref[...] = total


def state_kernel(where_ref, s0, s1, s2, s3, before_ref, out_ref, scratch):
    x = where_ref[0]
    heads, _, dk = before_ref.shape
    for k, part in enumerate((s0, s1, s2, s3)):
        scratch[lax.rem(x - k + 4, 4)] = part[...]
    for h in range(heads):
        row_state = jnp.concatenate([scratch[2 * h], scratch[2 * h + 1]], 0)
        moved = mm(row_state, before_ref[h, :dk, :])
        out_ref[h] = (moved + before_ref[h, dk:, :].astype(f32)).astype(bf16)


def gate_kernel(
    where_ref, s0, s1, s2, s3, before_ref, blend_ref, own_ref, gate_ref, gain_ref, out_ref,
    quarters, entry,
):
    state_kernel(where_ref, s0, s1, s2, s3, before_ref, entry, quarters)
    core = where_ref[1]
    heads, length, dk = own_ref.shape
    pairs, tokens = out_ref.shape[1], out_ref.shape[2]
    gain = gain_ref[...]
    for h in range(heads):
        mixed = own_ref[h] + mm_nt(blend_ref[h], entry[h])
        scale = lax.rsqrt(jnp.mean(mixed * mixed, 1, keepdims=True) + 1e-06)
        gates = gate_ref[:, h * dk : (h + 1) * dk].astype(f32)
        gated = (mixed * scale * gain * (gates * sigmoid(gates))).astype(bf16)
        for parity in range(2):
            mine = lax.rem(parity + core, 2)
            for pair in range(pairs):
                start = (2 * pair + parity) * tokens
                out_ref[mine, pair, :, h * dk : (h + 1) * dk] = gated[start : start + tokens]


def project_kernel(kept_ref, got_ref, own_ref, other_ref, out_ref):
    pairs, tokens, width = got_ref.shape
    rows = pairs * tokens
    total = mm(kept_ref[0].reshape(rows, width), own_ref[...])
    total = total + mm(got_ref[...].reshape(rows, width), other_ref[...])
    out_ref[...] = total.astype(bf16).reshape(out_ref.shape)


def route_kernel(topk, capacity, ids_ref, slot_ref, owner_ref, count_ref):
    tokens = ids_ref.shape[0]
    experts = count_ref.shape[0]

    def clear(i, carry):
        count_ref[i] = 0
        for r in range(capacity):
            owner_ref[i * capacity + r] = 0
        return carry

    lax.fori_loop(0, experts, clear, 0)

    def place(t, carry):
        for k in range(topk):
            expert = ids_ref[t, k]
            rank = count_ref[expert]
            count_ref[expert] = rank + 1
            slot = expert * capacity + rank
            slot_ref[t * topk + k] = slot
            owner_ref[slot] = t
        return carry

    lax.fori_loop(0, tokens, place, 0)


def dispatch_kernel(
    owner_ref, parts_ref, residual_ref, gain_ref, hidden_ref, out_ref, rows_ref, tiles_ref
):
    sources, tokens, width = parts_ref.shape
    lanes = out_ref.shape[2]
    cuts = width // lanes
    hidden = parts_ref[0].astype(f32)
    for s in range(1, sources):
        hidden = hidden + parts_ref[s].astype(f32)
    hidden = hidden + residual_ref[...].astype(f32)
    hidden_ref[...] = hidden
    scale = lax.rsqrt(jnp.mean(hidden * hidden, 1, keepdims=True) + 1e-06)
    normed = hidden * scale * gain_ref[...]
    for j in range(cuts):
        rows_ref[pl.ds(j, tokens, stride=cuts), :] = normed[:, j * lanes : (j + 1) * lanes]
    tiles_ref[...] = rows_ref[...].astype(bf16).reshape(tiles_ref.shape)
    unroll = 8

    def place(i, carry):
        for u in range(unroll):
            slot = i * unroll + u
            out_ref[slot] = tiles_ref[owner_ref[slot]]
        return carry

    lax.fori_loop(0, out_ref.shape[0] // unroll, place, 0)


def expert_kernel(rows_ref, gate_ref, up_ref, down_ref, out_ref, wide, flat):
    groups, _, capacity, cuts, lanes = rows_ref.shape
    rows = groups * capacity
    hidden_units = gate_ref.shape[3]
    depth = cuts * lanes
    wide[...] = rows_ref[...].astype(f32).reshape(rows * cuts, lanes)
    for j in range(cuts):
        flat[:, j * lanes : (j + 1) * lanes] = wide[pl.ds(j, rows, stride=cuts), :].astype(bf16)
    tokens = flat[...]
    first = mm(tokens, gate_ref[...].reshape(depth, hidden_units))
    second = mm(tokens, up_ref[...].reshape(depth, hidden_units))
    inner = (first * sigmoid(first) * second).astype(bf16)
    for j in range(0, cuts, 2):
        columns = []
        for packed in (down_ref[j, 0], down_ref[j + 1, 0]):
            columns.append(
                jnp.concatenate(
                    [packed[:, b : b + lanes] for b in range(0, hidden_units, lanes)], 0
                )
            )
        answer = mm(inner, jnp.concatenate(columns, 1))
        wide[pl.ds(j, rows, stride=cuts), :] = answer[:, :lanes]
        wide[pl.ds(j + 1, rows, stride=cuts), :] = answer[:, lanes:]
    out_ref[...] = wide[...].astype(bf16).reshape(out_ref.shape)


def combine_kernel(topk, slot_ref, weight_ref, back_ref, hidden_ref, out_ref, total):
    tokens, width = hidden_ref.shape
    cuts, lanes = back_ref.shape[1:]

    def add(t, carry):
        acc = jnp.zeros((cuts, lanes), f32)
        for k in range(topk):
            acc = acc + weight_ref[t, k] * back_ref[slot_ref[t * topk + k]].astype(f32)
        total[pl.ds(pl.multiple_of(t * cuts, cuts), cuts), :] = acc
        return carry

    lax.fori_loop(0, tokens, add, 0)
    for j in range(cuts):
        span = slice(j * lanes, (j + 1) * lanes)
        mixture = total[pl.ds(j, tokens, stride=cuts), :]
        out_ref[:, span] = (hidden_ref[:, span] + mixture).astype(bf16)


def shards(
    query_proj,
    key_proj,
    value_proj,
    output_gate,
    beta_logit,
    log_decay,
    norm_gain,
    out_weight,
    residual,
    moe_gain,
    expert_ids,
    route_weight,
    expert_gate,
    expert_up,
    expert_down,
):
    length, dk = query_proj.shape
    heads = beta_logit.shape[0]
    tokens, width = residual.shape
    experts_here, _, hidden_units = expert_gate.shape
    groups = lax.axis_size("ctx")
    topk = expert_ids.shape[1]
    capacity = 6
    lanes = 128
    cuts = width // lanes
    slots = groups * experts_here * capacity
    columns = 4
    pairs = lax.axis_size("exp") // 2
    rows = groups // columns
    place = lax.axis_index("ctx")
    x = lax.rem(place, columns)
    core = lax.rem(lax.axis_index("exp"), 2)
    where = jnp.stack([x, core]).astype(jnp.int32)

    def pair_swap(block):
        return lax.ppermute(block, "exp", [(i, i ^ 1) for i in range(2 * pairs)])

    def along_x(block, k):
        route = [
            (y * columns + i, y * columns + (i + k) % columns)
            for y in range(rows)
            for i in range(columns)
        ]
        return lax.ppermute(block, "ctx", route)

    def along_y(block, k):
        route = [(i, i + k * columns) for i in range((rows - k) * columns)]
        return lax.ppermute(block, "ctx", route)

    down_blocks = jnp.concatenate(
        [expert_down[:, b : b + lanes, :] for b in range(0, hidden_units, lanes)], 2
    )
    packed = jnp.concatenate([expert_gate, expert_up, down_blocks], 0)
    gathered = lax.all_gather(packed, "exp", axis=0)
    other_weight = pair_swap(out_weight)

    slot, owner = pl.pallas_call(
        functools.partial(route_kernel, topk, capacity),
        out_shape=(
            jax.ShapeDtypeStruct((tokens * topk,), jnp.int32),
            jax.ShapeDtypeStruct((slots,), jnp.int32),
        ),
        in_specs=[smem()],
        out_specs=(smem(), smem()),
        scratch_shapes=[pltpu.SMEM((groups * experts_here,), jnp.int32)],
        name="route",
    )(expert_ids)

    carry, blend, own = pl.pallas_call(
        functools.partial(scan_kernel, heads),
        out_shape=(
            jax.ShapeDtypeStruct((heads, 2 * dk, dk), bf16),
            jax.ShapeDtypeStruct((heads, length, dk), bf16),
            jax.ShapeDtypeStruct((heads, length, dk), f32),
        ),
        in_specs=[vmem()] * 5,
        out_specs=(vmem(),) * 3,
        compiler_params=params(32),
        cost_estimate=cost(2e9, 2e6),
        name="scan",
    )(query_proj, key_proj, value_proj, beta_logit, log_decay)

    maps = [carry] + [along_x(carry, k) for k in range(1, columns)]
    half = dk * heads // columns
    total, before = pl.pallas_call(
        row_kernel,
        out_shape=(
            jax.ShapeDtypeStruct((dk + half, dk), bf16),
            jax.ShapeDtypeStruct((heads, 2 * dk, dk), bf16),
        ),
        in_specs=[smem()] + [vmem()] * 4,
        out_specs=(vmem(), vmem()),
        name="row",
    )(where, *maps)
    window = follow(along_y(total, 1), along_y(total, 2))
    window = follow(window, along_y(window, 2))
    arrived = along_y(window[dk:], 4)
    quarter = (mm(arrived, window[:dk]) + window[dk:].astype(f32)).astype(bf16)
    quarters = [quarter] + [along_x(quarter, k) for k in range(1, columns)]

    gated = pl.pallas_call(
        gate_kernel,
        out_shape=jax.ShapeDtypeStruct((2, pairs, tokens, heads * dk), bf16),
        in_specs=[smem()] + [vmem()] * 9,
        out_specs=vmem(),
        scratch_shapes=[
            pltpu.VMEM((columns, half, dk), bf16),
            pltpu.VMEM((heads, dk, dk), bf16),
        ],
        compiler_params=params(32),
        cost_estimate=cost(1e8, 2e6),
        name="gate",
    )(where, *quarters, before, blend, own, output_gate, norm_gain.reshape(1, dk))
    got = pair_swap(gated[1])
    steps = 4
    wide = width // steps
    partial_sums = pl.pallas_call(
        project_kernel,
        grid=(steps,),
        out_shape=jax.ShapeDtypeStruct((pairs, tokens, width), bf16),
        in_specs=[
            pl.BlockSpec((1, pairs, tokens, heads * dk), lambda n: (0, 0, 0, 0)),
            pl.BlockSpec((pairs, tokens, heads * dk), lambda n: (0, 0, 0)),
            pl.BlockSpec((heads * dk, wide), lambda n: (0, n)),
            pl.BlockSpec((heads * dk, wide), lambda n: (0, n)),
        ],
        out_specs=pl.BlockSpec((pairs, tokens, wide), lambda n: (0, 0, n)),
        compiler_params=params(32),
        cost_estimate=cost(6e8, 4e6),
        name="project",
    )(gated, got, out_weight, other_weight)
    same_core = [[c + 2 * z for z in range(pairs)] for c in range(2)]
    parts = lax.all_to_all(
        partial_sums, "exp", 0, 0, tiled=True, axis_index_groups=same_core
    )

    hidden, outgoing = pl.pallas_call(
        dispatch_kernel,
        out_shape=(
            jax.ShapeDtypeStruct((tokens, width), f32),
            jax.ShapeDtypeStruct((slots, cuts, lanes), bf16),
        ),
        in_specs=[smem(), vmem(), vmem(), vmem()],
        out_specs=(vmem(), vmem()),
        scratch_shapes=[
            pltpu.VMEM((tokens * cuts, lanes), f32),
            pltpu.VMEM((tokens, cuts, lanes), bf16),
        ],
        compiler_params=params(32),
        cost_estimate=cost(1e6, 3e6),
        name="dispatch",
    )(owner, parts, residual, moe_gain.reshape(1, width))
    outgoing = outgoing.reshape(groups, experts_here, capacity, cuts, lanes)
    incoming = lax.all_to_all(outgoing, "ctx", 0, 0, tiled=True)

    shape = (groups, 1, capacity, cuts, lanes)
    weights = (2 * pairs, 1) + packed.shape[1:]
    answers = pl.pallas_call(
        expert_kernel,
        grid=(experts_here,),
        out_shape=jax.ShapeDtypeStruct(incoming.shape, bf16),
        in_specs=[
            pl.BlockSpec(shape, lambda e: (0, e, 0, 0, 0)),
            pl.BlockSpec(weights, lambda e: (0, e, 0, 0)),
            pl.BlockSpec(weights, lambda e: (0, experts_here + e, 0, 0)),
            pl.BlockSpec(weights, lambda e: (0, 2 * experts_here + e, 0, 0)),
        ],
        out_specs=pl.BlockSpec(shape, lambda e: (0, e, 0, 0, 0)),
        scratch_shapes=[
            pltpu.VMEM((groups * capacity * cuts, lanes), f32),
            pltpu.VMEM((groups * capacity, width), bf16),
        ],
        compiler_params=params(48),
        cost_estimate=cost(3e9, 16e6),
        name="experts",
    )(incoming, gathered, gathered, gathered)
    returned = lax.all_to_all(answers, "ctx", 0, 0, tiled=True).reshape(slots, cuts, lanes)

    return pl.pallas_call(
        functools.partial(combine_kernel, topk),
        out_shape=jax.ShapeDtypeStruct((tokens, width), bf16),
        in_specs=[smem(), smem(), vmem(), vmem()],
        out_specs=vmem(),
        scratch_shapes=[pltpu.VMEM((tokens * cuts, lanes), f32)],
        compiler_params=params(32),
        cost_estimate=cost(1e6, 3e6),
        name="combine",
    )(slot, route_weight, returned, hidden)


def solution(mesh):
    placed = (
        P("ctx", "exp"),
        P("ctx", "exp"),
        P("ctx", "exp"),
        P("ctx", "exp"),
        P("exp", "ctx"),
        P("exp", "ctx"),
        P(),
        P("exp", None),
        P(("ctx", "exp"), None),
        P(),
        P(("ctx", "exp"), None),
        P(("ctx", "exp"), None),
        P("ctx", "exp", None),
        P("ctx", "exp", None),
        P("ctx", None, "exp"),
    )
    return jax.shard_map(
        shards, mesh=mesh, in_specs=placed, out_specs=P(("ctx", "exp"), None), check_vma=False
    )
```

time: 772 us -> 234 us (0.30)
  the two profiles are of different devices: /device:TPU:4 before, /device:TPU:2 now
where the time goes in v1:
time: 234 us
  waiting for transfers between devices  73.5 us (31%)
  starting transfers between devices  63.3 us (27%)
  blocking collectives  49.9 us (21%)
  Pallas kernels  25.1 us (11%)
  between operations  13.7 us (6%)
  local copies, waits for them, and re-layouts  4.84 us (2%)
  other arithmetic  2.69 us (1%)
    all_to_all x1, blocking collectives, shards(): incoming = lax.all_to_all(outgoing, 'ctx', 0, 0, tiled=True)  49.9 us
    all_to_all x1, waiting for transfers between devices, shards(): lax.all_to_all(answers, 'ctx', 0, 0, tiled=True).reshape(slots, cuts, lanes)  38.4 us
    all_to_all x1, waiting for transfers between devices, shards(): lax.all_to_all(partial_sums, 'exp', 0, 0, tiled=True, axis_index_groups=s...  24.4 us
    ppermute x6, starting transfers between devices, along_x(): return lax.ppermute(block, 'ctx', route)  24.4 us
    ppermute x4, starting transfers between devices, along_y(): return lax.ppermute(block, 'ctx', route)  18.8 us
    all_to_all x1, starting transfers between devices, shards(): lax.all_to_all(partial_sums, 'exp', 0, 0, tiled=True, axis_index_groups=s...  10.6 us
    pallas_call x1, Pallas kernels, shards(): pl.pallas_call(expert_kernel, grid=(experts_here,), out_shape=jax.ShapeDt...  8.48 us
    ppermute x6, waiting for transfers between devices, along_x(): return lax.ppermute(block, 'ctx', route)  5.83 us
  transfers between devices with their start and end apart: 15, of which 8 were waited for; matrix products, arithmetic and copies ran while one was open for 1% of the time, Pallas kernels for 6%

profile of v1, /device:TPU:2, one launch (start us, length us, event | category | flops | bytes accessed | tf_op | source)
XLA Modules:
  0.0 233.5 jit_solution(7667584921552973188)
XLA Ops:
  6.5 0.0 all-gather.3.cloned.1.call-start
  6.6 1.0 fusion.5
  7.6 2.0 maximum_maximum_fusion
  9.6 0.0 all-gather.3.cloned.1.call-update
  9.7 0.0 copy-done.11
  9.7 0.0 copy-done.12
  9.7 0.0 copy-done.10
  9.7 0.0 copy-done.13
  9.7 0.0 copy-done.14
  9.7 0.0 copy-start
  9.7 0.0 copy-start.1
  9.7 0.0 copy-start.9
  9.7 3.1 %scan.1 = (bf16[2,256,128]{2,1,0:T(8,128)(2,1)S(1)}, bf16[2,512,128]{2,1,0:T(8,128)(2,1)S(1)}, f32[2,512,128]{2,1,0:T(8,128)S(1)}) custom-call(bf16[512,128]{1,0:T(8,128)(2,1)S(1)} %copy-done.11, bf16[512,128]{1,0:T(8,128)(2,1)S(1)} %copy-done.12, bf16[512,256]{1,0:T(8,128)(2,1)S(1)} %copy-done.10, f32[2,512]{1,0:T(2,128)S(1)} %copy-done.13, ...), custom_call_target="tpu_custom_call" | custom-call | flops 2000000000 | bytes 2000000 | tf_op jit(solution)/shard_map/scan/pallas_call | solution.py:385
  12.9 0.0 copy-start.4
  12.9 3.4 %collective-permute-start = (bf16[2,256,128]{2,1,0:T(8,128)(2,1)S(1)}, bf16[2,256,128]{2,1,0:T(8,128)(2,1)S(1)}, u32[]{:S(2)}, u32[]{:S(2)}) collective-permute-start(bf16[2,256,128]{2,1,0:T(8,128)(2,1)S(1)} %get-tuple-element.16.m0), channel_id=1, source_target_pairs={{0,16},{16,32},{32,48},{48,0},{64,80},{80,96},{96,112},{112,64},{1... | collective-permute-start | bytes 393224 | tf_op jit(solution)/shard_map/ppermute | solution.py:360
  16.3 8.4 %collective-permute-start.1 = (bf16[2,256,128]{2,1,0:T(8,128)(2,1)S(1)}, bf16[2,256,128]{2,1,0:T(8,128)(2,1)S(1)}, u32[]{:S(2)}, u32[]{:S(2)}) collective-permute-start(bf16[2,256,128]{2,1,0:T(8,128)(2,1)S(1)} %get-tuple-element.16.m0), channel_id=1, source_target_pairs={{0,32},{16,48},{32,0},{48,16},{64,96},{80,112},{96,64},{112,80},{1... | collective-permute-start | bytes 393224 | tf_op jit(solution)/shard_map/ppermute | solution.py:360
  24.7 1.9 collective-permute-start.2
  26.6 0.7 pad_add_fusion.where_ref
  27.3 0.0 collective-permute-done.m1
  27.3 0.3 collective-permute-done.1.m2
  27.6 3.9 %collective-permute-done.2.m3 = bf16[2,256,128]{2,1,0:T(8,128)(2,1)S(1)} collective-permute-done((bf16[2,256,128]{2,1,0:T(8,128)(2,1)S(1)}, bf16[2,256,128]{2,1,0:T(8,128)(2,1)S(1)}, u32[]{:S(2)}, u32[]{:S(2)}) %collective-permute-start.2) | collective-permute-done | bytes 131104 | tf_op jit(solution)/shard_map/ppermute | solution.py:360
  31.6 0.0 copy-done.15
  31.6 0.6 copy-done.17
  32.2 2.2 row.1
  34.4 1.3 collective-permute-start.4
  35.7 2.7 %collective-permute-start.3 = (bf16[192,128]{1,0:T(8,128)(2,1)}, bf16[192,128]{1,0:T(8,128)(2,1)S(1)}, u32[]{:S(2)}, u32[]{:S(2)}) collective-permute-start(bf16[192,128]{1,0:T(8,128)(2,1)} %get-tuple-element.17), channel_id=1, source_target_pairs={{0,128},{16,144},{32,160},{48,176},{64,192},{80,208},{96,224},{112... | collective-permute-start | bytes 147464 | tf_op jit(solution)/shard_map/ppermute | solution.py:364
  38.3 0.0 collective-permute-done.4
  38.4 2.0 collective-permute-done.3
  40.4 0.1 fusion.3
  40.6 5.1 %collective-permute-start.5 = (bf16[192,128]{1,0:T(8,128)(2,1)S(1)}, bf16[192,128]{1,0:T(8,128)(2,1)S(1)}, u32[]{:S(2)}, u32[]{:S(2)}) collective-permute-start(bf16[192,128]{1,0:T(8,128)(2,1)S(1)} %pad_maximum_fusion), channel_id=1, source_target_pairs={{0,128},{16,144},{32,160},{48,176},{64,192},{80,208},{96,224},{112... | collective-permute-start | bytes 147464 | tf_op jit(solution)/shard_map/ppermute | solution.py:364
  45.7 0.0 copy-done
  45.7 1.9 collective-permute-start.11
  47.7 0.0 collective-permute-done.5
  47.7 0.1 fusion.6
  47.8 9.7 %collective-permute-start.6 = (bf16[64,128]{1,0:T(8,128)(2,1)S(1)}, bf16[64,128]{1,0:T(8,128)(2,1)S(1)}, u32[]{:S(2)}, u32[]{:S(2)}) collective-permute-start(bf16[64,128]{1,0:T(8,128)(2,1)S(1)} %fusion.1), channel_id=1, source_target_pairs={{0,256},{16,272},{32,288},{48,304},{64,320},{80,336},{96,352},{112... | collective-permute-start | bytes 49160 | tf_op jit(solution)/shard_map/ppermute | solution.py:364
  57.5 1.4 collective-permute-done.6
  59.0 0.1 fusion.s0
  59.1 2.5 %collective-permute-start.7 = (bf16[64,128]{1,0:T(8,128)(2,1)S(1)}, bf16[64,128]{1,0:T(8,128)(2,1)S(1)}, u32[]{:S(2)}, u32[]{:S(2)}) collective-permute-start(bf16[64,128]{1,0:T(8,128)(2,1)S(1)} %fusion.s0), channel_id=1, source_target_pairs={{0,16},{16,32},{32,48},{48,0},{64,80},{80,96},{96,112},{112,64},{1... | collective-permute-start | bytes 49160 | tf_op jit(solution)/shard_map/ppermute | solution.py:360
  61.6 4.2 %collective-permute-start.8 = (bf16[64,128]{1,0:T(8,128)(2,1)S(1)}, bf16[64,128]{1,0:T(8,128)(2,1)S(1)}, u32[]{:S(2)}, u32[]{:S(2)}) collective-permute-start(bf16[64,128]{1,0:T(8,128)(2,1)S(1)} %fusion.s0), channel_id=1, source_target_pairs={{0,32},{16,48},{32,0},{48,16},{64,96},{80,112},{96,64},{112,80},{1... | collective-permute-start | bytes 49160 | tf_op jit(solution)/shard_map/ppermute | solution.py:360
  65.8 4.0 %collective-permute-start.9 = (bf16[64,128]{1,0:T(8,128)(2,1)S(1)}, bf16[64,128]{1,0:T(8,128)(2,1)S(1)}, u32[]{:S(2)}, u32[]{:S(2)}) collective-permute-start(bf16[64,128]{1,0:T(8,128)(2,1)S(1)} %fusion.s0), channel_id=1, source_target_pairs={{0,48},{16,0},{32,16},{48,32},{64,112},{80,64},{96,80},{112,96},{1... | collective-permute-start | bytes 49160 | tf_op jit(solution)/shard_map/ppermute | solution.py:360
  69.8 0.0 collective-permute-done.7.s1
  69.8 0.0 collective-permute-done.8.s2
  69.8 1.6 collective-permute-done.9.s3
  71.4 1.0 copy-done.3
  72.4 0.7 copy-done.6
  73.0 1.1 gate.1.kept_ref
  74.2 1.9 collective-permute-start.10
  76.1 1.3 collective-permute-done.10.got_ref
  77.5 0.0 collective-permute-done.11.other_ref
  77.5 2.5 %project.1 = bf16[8,32,2048]{2,1,0:T(8,128)(2,1)} custom-call(bf16[2,8,32,256]{3,2,1,0:T(8,128)(2,1)S(1)} %gate.1.kept_ref, bf16[8,32,256]{2,1,0:T(8,128)(2,1)S(1)} %collective-permute-done.10.got_ref, bf16[256,2048]{1,0:T(8,128)(2,1)S(1)} %copy-done, bf16[256,2048]{1,0:T(8,128)(2,1)S(1)} %collective-permute-done.11.other_ref), custom_call_target="tpu_custom_call" | custom-call | flops 600000000 | bytes 4000000 | tf_op jit(solution)/shard_map/project/pallas_call | solution.py:433
  79.9 10.6 %all-to-all-start = ((bf16[8,32,2048]{2,1,0:T(8,128)(2,1)}), bf16[8,32,2048]{2,1,0:T(8,128)(2,1)S(1)}, u32[]{:S(2)}, u32[]{:S(2)}) async-start(bf16[8,32,2048]{2,1,0:T(8,128)(2,1)} %project.1), calls=%async_computation | async-start | bytes 2097152 | tf_op jit(solution)/shard_map/all_to_all | solution.py:449
  90.5 0.7 copy.18.ids_ref
  91.2 3.9 %route.1 = (s32[320]{0:T(512)}, s32[384]{0:T(512)}) custom-call(s32[32,10]{1,0:T(8,128)} %copy.18.ids_ref), custom_call_target="tpu_custom_call" | custom-call | tf_op jit(solution)/shard_map/route/pallas_call | solution.py:373
  95.1 24.4 %all-to-all-done.parts_ref = bf16[8,32,2048]{2,1,0:T(8,128)(2,1)S(1)} async-done(((bf16[8,32,2048]{2,1,0:T(8,128)(2,1)}), bf16[8,32,2048]{2,1,0:T(8,128)(2,1)S(1)}, u32[]{:S(2)}, u32[]{:S(2)}) %all-to-all-start) | async-done | bytes 1048608 | tf_op jit(solution)/shard_map/all_to_all | solution.py:449
  119.6 0.0 copy-done.2
  119.6 0.7 copy-done.8
  120.3 1.5 dispatch.1
  121.8 49.9 %all_to_all.15.rows_ref = bf16[32,2,6,16,128]{4,3,2,1,0:T(8,128)(2,1)S(1)} all-to-all(bf16[32,2,6,16,128]{4,3,2,1,0:T(8,128)(2,1)S(1)} %bitcast.13), channel_id=1, replica_groups=mesh['ctx'=32,'exp'=16] {'ctx'}, dimensions={0} | all-to-all | bytes 3145728 | tf_op jit(solution)/shard_map/all_to_all | solution.py:470
  171.6 8.5 %experts.1 = bf16[32,2,6,16,128]{4,3,2,1,0:T(8,128)(2,1)} custom-call(bf16[32,2,6,16,128]{4,3,2,1,0:T(8,128)(2,1)S(1)} %all_to_all.15.rows_ref, bf16[16,6,128,512]{3,2,1,0:T(8,128)(2,1)} %bitcast.16, bf16[16,6,128,512]{3,2,1,0:T(8,128)(2,1)} %bitcast.17, bf16[16,6,128,512]{3,2,1,0:T(8,128)(2,1)} %bitcast.18), custom_call_target="tpu_custom_call" | custom-call | flops 3000000000 | bytes 16000000 | tf_op jit(solution)/shard_map/experts/pallas_call | solution.py:474
  180.1 5.7 %all-to-all-start.2 = ((bf16[32,2,6,16,128]{4,3,2,1,0:T(8,128)(2,1)}), bf16[32,2,6,16,128]{4,3,2,1,0:T(8,128)(2,1)S(1)}, u32[]{:S(2)}, u32[]{:S(2)}) async-start(bf16[32,2,6,16,128]{4,3,2,1,0:T(8,128)(2,1)} %experts.1), calls=%async_computation.2 | async-start | bytes 3145728 | tf_op jit(solution)/shard_map/all_to_all | solution.py:493
  185.8 0.0 copy-done.19
  185.8 0.1 copy.19.weight_ref
  185.9 38.4 %all-to-all-done.2 = bf16[32,2,6,16,128]{4,3,2,1,0:T(8,128)(2,1)S(1)} async-done(((bf16[32,2,6,16,128]{4,3,2,1,0:T(8,128)(2,1)}), bf16[32,2,6,16,128]{4,3,2,1,0:T(8,128)(2,1)S(1)}, u32[]{:S(2)}, u32[]{:S(2)}) %all-to-all-start.2) | async-done | bytes 1572896 | tf_op jit(solution)/shard_map/all_to_all | solution.py:493
  224.4 2.3 combine.1
  (29 shorter events, 0.1 us)
Async XLA Ops:
  6.5 3.1 %copy-start.11 = (bf16[512,128]{1,0:T(8,128)(2,1)S(1)}, bf16[512,128]{1,0:T(8,128)(2,1)}, u32[]{:S(2)}) copy-start(bf16[512,128]{1,0:T(8,128)(2,1)} %q_ref.1) | copy-start | bytes 393220
  6.5 3.1 %copy-start.12 = (bf16[512,128]{1,0:T(8,128)(2,1)S(1)}, bf16[512,128]{1,0:T(8,128)(2,1)}, u32[]{:S(2)}) copy-start(bf16[512,128]{1,0:T(8,128)(2,1)} %k_ref.1) | copy-start | bytes 393220
  6.5 3.1 %copy-start.10 = (bf16[512,256]{1,0:T(8,128)(2,1)S(1)}, bf16[512,256]{1,0:T(8,128)(2,1)}, u32[]{:S(2)}) copy-start(bf16[512,256]{1,0:T(8,128)(2,1)} %v_ref.1) | copy-start | bytes 786436
  6.5 3.1 %copy-start.13 = (f32[2,512]{1,0:T(2,128)S(1)}, f32[2,512]{1,0:T(2,128)}, u32[]{:S(2)}) copy-start(f32[2,512]{1,0:T(2,128)} %beta_ref.1) | copy-start | bytes 12292
  6.5 3.2 %copy-start.14 = (f32[2,512]{1,0:T(2,128)S(1)}, f32[2,512]{1,0:T(2,128)}, u32[]{:S(2)}) copy-start(f32[2,512]{1,0:T(2,128)} %log_ref.1) | copy-start | bytes 12292
  6.5 165.1 %all-gather.3.cloned.1.call-start = ((), (), s32[]{:S(2)}) async-start(), calls=%async_computation.3 | async-start | bytes 13369344 | tf_op jit(solution)/shard_map/all_gather | solution.py:370
  9.7 36.0 %copy-start = (bf16[256,2048]{1,0:T(8,128)(2,1)S(1)}, bf16[256,2048]{1,0:T(8,128)(2,1)}, u32[]{:S(2)}) copy-start(bf16[256,2048]{1,0:T(8,128)(2,1)} %own_ref.1) | copy-start | bytes 3145732
  9.7 61.7 %copy-start.1 = (bf16[512,256]{1,0:T(8,128)(2,1)S(1)}, bf16[512,256]{1,0:T(8,128)(2,1)}, u32[]{:S(2)}) copy-start(bf16[512,256]{1,0:T(8,128)(2,1)} %gate_ref.1) | copy-start | bytes 786436
  9.7 61.7 %copy-start.9 = (f32[128]{0:T(128)S(1)}, f32[128]{0:T(128)}, u32[]{:S(2)}) copy-start(f32[128]{0:T(128)} %param.21) | copy-start | bytes 1540
  12.9 18.7 %copy-start.4 = (bf16[2,256,128]{2,1,0:T(8,128)(2,1)}, bf16[2,256,128]{2,1,0:T(8,128)(2,1)S(1)}, u32[]{:S(2)}) copy-start(bf16[2,256,128]{2,1,0:T(8,128)(2,1)S(1)} %get-tuple-element.16.m0) | copy-start | bytes 393220
  12.9 14.4 %collective-permute-start = (bf16[2,256,128]{2,1,0:T(8,128)(2,1)S(1)}, bf16[2,256,128]{2,1,0:T(8,128)(2,1)S(1)}, u32[]{:S(2)}, u32[]{:S(2)}) collective-permute-start(bf16[2,256,128]{2,1,0:T(8,128)(2,1)S(1)} %get-tuple-element.16.m0), channel_id=1, source_target_pairs={{0,16},{16,32},{32,48},{48,0},{64,80},{80,96},{96,112},{112,64},{1... | collective-permute-start | bytes 393224 | tf_op jit(solution)/shard_map/ppermute | solution.py:360
  16.3 11.3 %collective-permute-start.1 = (bf16[2,256,128]{2,1,0:T(8,128)(2,1)S(1)}, bf16[2,256,128]{2,1,0:T(8,128)(2,1)S(1)}, u32[]{:S(2)}, u32[]{:S(2)}) collective-permute-start(bf16[2,256,128]{2,1,0:T(8,128)(2,1)S(1)} %get-tuple-element.16.m0), channel_id=1, source_target_pairs={{0,32},{16,48},{32,0},{48,16},{64,96},{80,112},{96,64},{112,80},{1... | collective-permute-start | bytes 393224 | tf_op jit(solution)/shard_map/ppermute | solution.py:360
  24.7 6.9 %collective-permute-start.2 = (bf16[2,256,128]{2,1,0:T(8,128)(2,1)S(1)}, bf16[2,256,128]{2,1,0:T(8,128)(2,1)S(1)}, u32[]{:S(2)}, u32[]{:S(2)}) collective-permute-start(bf16[2,256,128]{2,1,0:T(8,128)(2,1)S(1)} %get-tuple-element.16.m0), channel_id=1, source_target_pairs={{0,48},{16,0},{32,16},{48,32},{64,112},{80,64},{96,80},{112,96},{1... | collective-permute-start | bytes 393224 | tf_op jit(solution)/shard_map/ppermute | solution.py:360
  27.3 4.3 %copy-start.15 = (bf16[2,256,128]{2,1,0:T(8,128)(2,1)}, bf16[2,256,128]{2,1,0:T(8,128)(2,1)S(1)}, u32[]{:S(2)}) copy-start(bf16[2,256,128]{2,1,0:T(8,128)(2,1)S(1)} %collective-permute-done.m1) | copy-start | bytes 393220
  27.6 3.9 %copy-start.16 = (bf16[2,256,128]{2,1,0:T(8,128)(2,1)}, bf16[2,256,128]{2,1,0:T(8,128)(2,1)S(1)}, u32[]{:S(2)}) copy-start(bf16[2,256,128]{2,1,0:T(8,128)(2,1)S(1)} %collective-permute-done.1.m2) | copy-start | bytes 393220
  31.6 0.6 copy-start.17
  34.4 4.0 %collective-permute-start.4 = (bf16[192,128]{1,0:T(8,128)(2,1)}, bf16[192,128]{1,0:T(8,128)(2,1)S(1)}, u32[]{:S(2)}, u32[]{:S(2)}) collective-permute-start(bf16[192,128]{1,0:T(8,128)(2,1)} %get-tuple-element.17), channel_id=1, source_target_pairs={{0,64},{16,80},{32,96},{48,112},{64,128},{80,144},{96,160},{112,17... | collective-permute-start | bytes 147464 | tf_op jit(solution)/shard_map/ppermute | solution.py:364
  35.7 4.7 %collective-permute-start.3 = (bf16[192,128]{1,0:T(8,128)(2,1)}, bf16[192,128]{1,0:T(8,128)(2,1)S(1)}, u32[]{:S(2)}, u32[]{:S(2)}) collective-permute-start(bf16[192,128]{1,0:T(8,128)(2,1)} %get-tuple-element.17), channel_id=1, source_target_pairs={{0,128},{16,144},{32,160},{48,176},{64,192},{80,208},{96,224},{112... | collective-permute-start | bytes 147464 | tf_op jit(solution)/shard_map/ppermute | solution.py:364
  40.6 7.1 %collective-permute-start.5 = (bf16[192,128]{1,0:T(8,128)(2,1)S(1)}, bf16[192,128]{1,0:T(8,128)(2,1)S(1)}, u32[]{:S(2)}, u32[]{:S(2)}) collective-permute-start(bf16[192,128]{1,0:T(8,128)(2,1)S(1)} %pad_maximum_fusion), channel_id=1, source_target_pairs={{0,128},{16,144},{32,160},{48,176},{64,192},{80,208},{96,224},{112... | collective-permute-start | bytes 147464 | tf_op jit(solution)/shard_map/ppermute | solution.py:364
  45.7 31.7 %collective-permute-start.11 = (bf16[256,2048]{1,0:T(8,128)(2,1)S(1)}, bf16[256,2048]{1,0:T(8,128)(2,1)S(1)}, u32[]{:S(2)}, u32[]{:S(2)}) collective-permute-start(bf16[256,2048]{1,0:T(8,128)(2,1)S(1)} %copy-done), channel_id=1, source_target_pairs={{0,1},{1,0},{2,3},{3,2},{4,5},{5,4},{6,7},{7,6},{8,9},{9,8},{10,11... | collective-permute-start | bytes 3145736 | tf_op jit(solution)/shard_map/ppermute | solution.py:352
  47.8 11.1 %collective-permute-start.6 = (bf16[64,128]{1,0:T(8,128)(2,1)S(1)}, bf16[64,128]{1,0:T(8,128)(2,1)S(1)}, u32[]{:S(2)}, u32[]{:S(2)}) collective-permute-start(bf16[64,128]{1,0:T(8,128)(2,1)S(1)} %fusion.1), channel_id=1, source_target_pairs={{0,256},{16,272},{32,288},{48,304},{64,320},{80,336},{96,352},{112... | collective-permute-start | bytes 49160 | tf_op jit(solution)/shard_map/ppermute | solution.py:364
  59.1 10.7 %collective-permute-start.7 = (bf16[64,128]{1,0:T(8,128)(2,1)S(1)}, bf16[64,128]{1,0:T(8,128)(2,1)S(1)}, u32[]{:S(2)}, u32[]{:S(2)}) collective-permute-start(bf16[64,128]{1,0:T(8,128)(2,1)S(1)} %fusion.s0), channel_id=1, source_target_pairs={{0,16},{16,32},{32,48},{48,0},{64,80},{80,96},{96,112},{112,64},{1... | collective-permute-start | bytes 49160 | tf_op jit(solution)/shard_map/ppermute | solution.py:360
  61.6 8.3 %collective-permute-start.8 = (bf16[64,128]{1,0:T(8,128)(2,1)S(1)}, bf16[64,128]{1,0:T(8,128)(2,1)S(1)}, u32[]{:S(2)}, u32[]{:S(2)}) collective-permute-start(bf16[64,128]{1,0:T(8,128)(2,1)S(1)} %fusion.s0), channel_id=1, source_target_pairs={{0,32},{16,48},{32,0},{48,16},{64,96},{80,112},{96,64},{112,80},{1... | collective-permute-start | bytes 49160 | tf_op jit(solution)/shard_map/ppermute | solution.py:360
  65.8 5.6 %collective-permute-start.9 = (bf16[64,128]{1,0:T(8,128)(2,1)S(1)}, bf16[64,128]{1,0:T(8,128)(2,1)S(1)}, u32[]{:S(2)}, u32[]{:S(2)}) collective-permute-start(bf16[64,128]{1,0:T(8,128)(2,1)S(1)} %fusion.s0), channel_id=1, source_target_pairs={{0,48},{16,0},{32,16},{48,32},{64,112},{80,64},{96,80},{112,96},{1... | collective-permute-start | bytes 49160 | tf_op jit(solution)/shard_map/ppermute | solution.py:360
  71.4 1.0 copy-start.3
  72.4 0.7 copy-start.6
  74.2 3.2 %collective-permute-start.10 = (bf16[8,32,256]{2,1,0:T(8,128)(2,1)S(1)}, bf16[8,32,256]{2,1,0:T(8,128)(2,1)S(1)}, u32[]{:S(2)}, u32[]{:S(2)}) collective-permute-start(bf16[8,32,256]{2,1,0:T(8,128)(2,1)S(1)} %slice_bitcast_fusion), channel_id=1, source_target_pairs={{0,1},{1,0},{2,3},{3,2},{4,5},{5,4},{6,7},{7,6},{8,9},{9,8},{10,11... | collective-permute-start | bytes 393224 | tf_op jit(solution)/shard_map/ppermute | solution.py:352
  79.9 10.6 %copy-start.18 = (s32[32,10]{0,1:T(8,128)S(1)}, s32[32,10]{0,1:T(8,128)}, u32[]{:S(2)}) copy-start(s32[32,10]{0,1:T(8,128)} %param.25) | copy-start | bytes 3844
  79.9 39.6 %copy-start.2 = (bf16[32,2048]{1,0:T(8,128)(2,1)S(1)}, bf16[32,2048]{1,0:T(8,128)(2,1)}, u32[]{:S(2)}) copy-start(bf16[32,2048]{1,0:T(8,128)(2,1)} %residual_ref.1) | copy-start | bytes 393220
  79.9 39.6 %copy-start.5 = (f32[2048]{0:T(1024)S(1)}, f32[2048]{0:T(1024)}, u32[]{:S(2)}) copy-start(f32[2048]{0:T(1024)} %param.24) | copy-start | bytes 24580
  79.9 39.6 %all-to-all-start = ((bf16[8,32,2048]{2,1,0:T(8,128)(2,1)}), bf16[8,32,2048]{2,1,0:T(8,128)(2,1)S(1)}, u32[]{:S(2)}, u32[]{:S(2)}) async-start(bf16[8,32,2048]{2,1,0:T(8,128)(2,1)} %project.1), calls=%async_computation | async-start | bytes 2097152 | tf_op jit(solution)/shard_map/all_to_all | solution.py:449
  119.6 0.7 copy-start.8
  180.1 5.7 %copy-start.19 = (f32[32,10]{0,1:T(8,128)S(1)}, f32[32,10]{0,1:T(8,128)}, u32[]{:S(2)}) copy-start(f32[32,10]{0,1:T(8,128)} %param.26) | copy-start | bytes 3844
  180.1 44.2 %copy-start.7 = (s32[320]{0:T(512)S(1)}, s32[320]{0:T(512)}, u32[]{:S(2)}) copy-start(s32[320]{0:T(512)} %get-tuple-element.14.slot_ref) | copy-start | bytes 3844
  180.1 44.2 %all-to-all-start.2 = ((bf16[32,2,6,16,128]{4,3,2,1,0:T(8,128)(2,1)}), bf16[32,2,6,16,128]{4,3,2,1,0:T(8,128)(2,1)S(1)}, u32[]{:S(2)}, u32[]{:S(2)}) async-start(bf16[32,2,6,16,128]{4,3,2,1,0:T(8,128)(2,1)} %experts.1), calls=%async_computation.2 | async-start | bytes 3145728 | tf_op jit(solution)/shard_map/all_to_all | solution.py:493
Sparse Core Ops, SparseCore 0:
  9.8 83.7 all-gather.2

commit v2 on v1

--- a/solution.py
+++ b/solution.py
@@ -21,6 +21,10 @@
 
 def smem():
     return pl.BlockSpec(memory_space=SMEM)
+
+
+def anywhere():
+    return pl.BlockSpec(memory_space=pl.ANY)
 
 
 def params(mib):
@@ -48,7 +52,31 @@
     return 1.0 / (1.0 + jnp.exp(-value))
 
 
-def scan_kernel(heads, q_ref, k_ref, v_ref, beta_ref, log_ref, carry_ref, blend_ref, own_ref):
+def start_copies(moves, sems):
+    copies = [pltpu.make_async_copy(a, b, sems.at[i]) for i, (a, b) in enumerate(moves)]
+    for copy in copies:
+        copy.start()
+    return copies
+
+
+def pack_down(down_ref, packed_ref):
+    experts, depth, lanes = down_ref.shape
+    return [
+        (down_ref.at[e, b : b + lanes, :], packed_ref.at[e, :, b : b + lanes])
+        for e in range(experts)
+        for b in range(0, depth, lanes)
+    ]
+
+
+def scan_kernel(
+    heads, q_ref, k_ref, v_ref, beta_ref, log_ref, gate_ref, up_ref,
+    carry_ref, blend_ref, own_ref, packed_ref, sems,
+):
+    experts = gate_ref.shape[0]
+    copies = start_copies(
+        [(gate_ref, packed_ref.at[0:experts]), (up_ref, packed_ref.at[experts : 2 * experts])],
+        sems,
+    )
     length, dk = q_ref.shape
     count = length // BLOCK
     row = lax.broadcasted_iota(jnp.int32, (BLOCK, BLOCK), 0)
@@ -122,7 +150,7 @@
             low = state.astype(bf16)
             out = mm(p["queries"] - p["seen"][:, :dk], low)
             blend_ref[h, span, :] = out[:, :dk].astype(bf16)
-            own_ref[h, span, :] = out[:, dk:] + p["seen"][:, dk:]
+            own_ref[h, span, :] = (out[:, dk:] + p["seen"][:, dk:]).astype(bf16)
             push = p["push"]
             moved = mm(push[:, :dk], low)
             states[h] = jnp.concatenate(
@@ -133,8 +161,12 @@
                 1,
             )
     for h in range(heads):
-        carry_ref[h, :dk, :] = jnp.transpose(states[h][:, :dk]).astype(bf16)
-        carry_ref[h, dk:, :] = jnp.transpose(states[h][:, dk:]).astype(bf16)
+        for part in range(2):
+            turned = jnp.transpose(states[h][:, part * dk : (part + 1) * dk]).astype(bf16)
+            for place in range(carry_ref.shape[0]):
+                carry_ref[place, h, part * dk : (part + 1) * dk, :] = turned
+    for copy in copies:
+        copy.wait()
 
 
 def follow(late, early):
@@ -143,18 +175,16 @@
     return jnp.concatenate([moved[:dk], moved[dk:] + late[dk:].astype(f32)], 0).astype(bf16)
 
 
-def row_kernel(where_ref, m0, m1, m2, m3, total_ref, before_ref):
-    x = where_ref[0]
-    maps = (m0, m1, m2, m3)
-    heads, _, dk = m0.shape
-    half = dk * heads // 4
-    for place in range(4):
+def row_kernel(maps_ref, total_ref, before_ref):
+    columns, heads, _, dk = maps_ref.shape
+    x = lax.rem(lax.axis_index("ctx"), columns)
+    half = dk * heads // columns
+    for place in range(columns):
 
         @pl.when(x == place)
         def _():
-            ordered = [maps[(place - j) % 4] for j in range(4)]
             for h in range(heads):
-                parts = [ordered[j][h] for j in range(4)]
+                parts = [maps_ref[j, h] for j in range(columns)]
                 prefix = parts[0]
                 for j in range(1, place):
                     prefix = follow(parts[j], prefix)
@@ -166,39 +196,43 @@
                         [jnp.where(eye, 1.0, 0.0), jnp.zeros((dk, dk), f32)], 0
                     ).astype(bf16)
                 before_ref[h] = prefix
-                if h == place // 2:
-                    low = dk + (place % 2) * half
+                if h == place * heads // columns:
+                    low = dk + (place % (columns // heads)) * half
                     cut = [
                         jnp.concatenate([part[:dk], part[low : low + half]], 0) for part in parts
                     ]
                     total = cut[0]
-                    for j in range(1, 4):
+                    for j in range(1, columns):
                         total = follow(cut[j], total)
-                    total_ref[...] = total
-
-
-def state_kernel(where_ref, s0, s1, s2, s3, before_ref, out_ref, scratch):
-    x = where_ref[0]
-    heads, _, dk = before_ref.shape
-    for k, part in enumerate((s0, s1, s2, s3)):
-        scratch[lax.rem(x - k + 4, 4)] = part[...]
-    for h in range(heads):
-        row_state = jnp.concatenate([scratch[2 * h], scratch[2 * h + 1]], 0)
-        moved = mm(row_state, before_ref[h, :dk, :])
-        out_ref[h] = (moved + before_ref[h, dk:, :].astype(f32)).astype(bf16)
+                    for row in range(total_ref.shape[0]):
+                        total_ref[row] = total
+
+
+def column_kernel(totals_ref, out_ref):
+    dk = totals_ref.shape[2]
+    y = lax.axis_index("ctx") // out_ref.shape[0]
+
+    state = jnp.zeros(out_ref.shape[1:], f32)
+    for j in range(totals_ref.shape[0] - 1):
+        moved = mm(state, totals_ref[j, :dk, :]) + totals_ref[j, dk:, :].astype(f32)
+        state = jnp.where(j < y, moved, state)
+    state = state.astype(bf16)
+    for place in range(out_ref.shape[0]):
+        out_ref[place] = state
 
 
 def gate_kernel(
-    where_ref, s0, s1, s2, s3, before_ref, blend_ref, own_ref, gate_ref, gain_ref, out_ref,
-    quarters, entry,
+    quarters_ref, before_ref, blend_ref, own_ref, gate_ref, gain_ref, out_ref
 ):
-    state_kernel(where_ref, s0, s1, s2, s3, before_ref, entry, quarters)
-    core = where_ref[1]
+    core = lax.rem(lax.axis_index("exp"), 2)
     heads, length, dk = own_ref.shape
     pairs, tokens = out_ref.shape[1], out_ref.shape[2]
+    share = quarters_ref.shape[0] // heads
     gain = gain_ref[...]
     for h in range(heads):
-        mixed = own_ref[h] + mm_nt(blend_ref[h], entry[h])
+        row_state = jnp.concatenate([quarters_ref[share * h + i] for i in range(share)], 0)
+        entry = mm(row_state, before_ref[h, :dk, :]) + before_ref[h, dk:, :].astype(f32)
+        mixed = own_ref[h].astype(f32) + mm_nt(blend_ref[h], entry)
         scale = lax.rsqrt(jnp.mean(mixed * mixed, 1, keepdims=True) + 1e-06)
         gates = gate_ref[:, h * dk : (h + 1) * dk].astype(f32)
         gated = (mixed * scale * gain * (gates * sigmoid(gates))).astype(bf16)
@@ -243,8 +277,10 @@
 
 
 def dispatch_kernel(
-    owner_ref, parts_ref, residual_ref, gain_ref, hidden_ref, out_ref, rows_ref, tiles_ref
+    owner_ref, parts_ref, residual_ref, gain_ref, down_ref, after_ref,
+    hidden_ref, out_ref, packed_ref, rows_ref, tiles_ref, sems,
 ):
+    copies = start_copies(pack_down(down_ref, packed_ref), sems)
     sources, tokens, width = parts_ref.shape
     lanes = out_ref.shape[2]
     cuts = width // lanes
@@ -267,32 +303,51 @@
         return carry
 
     lax.fori_loop(0, out_ref.shape[0] // unroll, place, 0)
-
-
-def expert_kernel(rows_ref, gate_ref, up_ref, down_ref, out_ref, wide, flat):
-    groups, _, capacity, cuts, lanes = rows_ref.shape
+    for copy in copies:
+        copy.wait()
+
+
+def expert_kernel(rows_ref, first_ref, last_ref, out_ref, first_vmem, last_vmem, sems, *scratch):
+    groups, experts, capacity, cuts, lanes = rows_ref.shape
+    moves = []
+    for e in range(experts):
+        moves.append((first_ref.at[:, e], first_vmem.at[:, e]))
+        moves.append((first_ref.at[:, experts + e], first_vmem.at[:, experts + e]))
+        moves.append((last_ref.at[:, e], last_vmem.at[:, e]))
+    copies = start_copies(moves, sems)
     rows = groups * capacity
-    hidden_units = gate_ref.shape[3]
+    hidden_units = first_ref.shape[3]
     depth = cuts * lanes
-    wide[...] = rows_ref[...].astype(f32).reshape(rows * cuts, lanes)
-    for j in range(cuts):
-        flat[:, j * lanes : (j + 1) * lanes] = wide[pl.ds(j, rows, stride=cuts), :].astype(bf16)
-    tokens = flat[...]
-    first = mm(tokens, gate_ref[...].reshape(depth, hidden_units))
-    second = mm(tokens, up_ref[...].reshape(depth, hidden_units))
-    inner = (first * sigmoid(first) * second).astype(bf16)
-    for j in range(0, cuts, 2):
-        columns = []
-        for packed in (down_ref[j, 0], down_ref[j + 1, 0]):
-            columns.append(
-                jnp.concatenate(
-                    [packed[:, b : b + lanes] for b in range(0, hidden_units, lanes)], 0
+    wide_in, wide_out, flat = scratch[:experts], scratch[experts : 2 * experts], scratch[2 * experts :]
+    for e in range(experts):
+        wide_in[e][...] = rows_ref[:, e].astype(f32).reshape(rows * cuts, lanes)
+        for j in range(cuts):
+            part = wide_in[e][pl.ds(j, rows, stride=cuts), :]
+            flat[e][:, j * lanes : (j + 1) * lanes] = part.astype(bf16)
+    for e in range(experts):
+        tokens = flat[e][...]
+        copies[3 * e].wait()
+        first = mm(tokens, first_vmem[:, e].reshape(depth, hidden_units))
+        copies[3 * e + 1].wait()
+        second = mm(tokens, first_vmem[:, experts + e].reshape(depth, hidden_units))
+        inner = (first * sigmoid(first) * second).astype(bf16)
+        copies[3 * e + 2].wait()
+        for j in range(0, cuts, 2):
+            columns = []
+            for k in (j, j + 1):
+                columns.append(
+                    jnp.concatenate(
+                        [
+                            last_vmem[k, e, :, b : b + lanes]
+                            for b in range(0, hidden_units, lanes)
+                        ],
+                        0,
+                    )
                 )
-            )
-        answer = mm(inner, jnp.concatenate(columns, 1))
-        wide[pl.ds(j, rows, stride=cuts), :] = answer[:, :lanes]
-        wide[pl.ds(j + 1, rows, stride=cuts), :] = answer[:, lanes:]
-    out_ref[...] = wide[...].astype(bf16).reshape(out_ref.shape)
+            answer = mm(inner, jnp.concatenate(columns, 1))
+            wide_out[e][pl.ds(j, rows, stride=cuts), :] = answer[:, :lanes]
+            wide_out[e][pl.ds(j + 1, rows, stride=cuts), :] = answer[:, lanes:]
+        out_ref[:, e] = wide_out[e][...].astype(bf16).reshape(groups, capacity, cuts, lanes)
 
 
 def combine_kernel(topk, slot_ref, weight_ref, back_ref, hidden_ref, out_ref, total):
@@ -306,7 +361,7 @@
         total[pl.ds(pl.multiple_of(t * cuts, cuts), cuts), :] = acc
         return carry
 
-    lax.fori_loop(0, tokens, add, 0)
+    lax.fori_loop(0, tokens, add, 0, unroll=2)
     for j in range(cuts):
         span = slice(j * lanes, (j + 1) * lanes)
         mixture = total[pl.ds(j, tokens, stride=cuts), :]
@@ -343,31 +398,16 @@
     columns = 4
     pairs = lax.axis_size("exp") // 2
     rows = groups // columns
-    place = lax.axis_index("ctx")
-    x = lax.rem(place, columns)
-    core = lax.rem(lax.axis_index("exp"), 2)
-    where = jnp.stack([x, core]).astype(jnp.int32)
+    along_x = [[y * columns + i for i in range(columns)] for y in range(rows)]
+    along_y = [[y * columns + i for y in range(rows)] for i in range(columns)]
+    half = dk * heads // columns
 
     def pair_swap(block):
         return lax.ppermute(block, "exp", [(i, i ^ 1) for i in range(2 * pairs)])
 
-    def along_x(block, k):
-        route = [
-            (y * columns + i, y * columns + (i + k) % columns)
-            for y in range(rows)
-            for i in range(columns)
-        ]
-        return lax.ppermute(block, "ctx", route)
-
-    def along_y(block, k):
-        route = [(i, i + k * columns) for i in range((rows - k) * columns)]
-        return lax.ppermute(block, "ctx", route)
-
-    down_blocks = jnp.concatenate(
-        [expert_down[:, b : b + lanes, :] for b in range(0, hidden_units, lanes)], 2
-    )
-    packed = jnp.concatenate([expert_gate, expert_up, down_blocks], 0)
-    gathered = lax.all_gather(packed, "exp", axis=0)
+    def exchange(blocks, groups):
+        return lax.all_to_all(blocks, "ctx", 0, 0, tiled=True, axis_index_groups=groups)
+
     other_weight = pair_swap(out_weight)
 
     slot, owner = pl.pallas_call(
@@ -382,66 +422,67 @@
         name="route",
     )(expert_ids)
 
-    carry, blend, own = pl.pallas_call(
+    carry, blend, own, packed = pl.pallas_call(
         functools.partial(scan_kernel, heads),
         out_shape=(
-            jax.ShapeDtypeStruct((heads, 2 * dk, dk), bf16),
+            jax.ShapeDtypeStruct((columns, heads, 2 * dk, dk), bf16),
             jax.ShapeDtypeStruct((heads, length, dk), bf16),
-            jax.ShapeDtypeStruct((heads, length, dk), f32),
+            jax.ShapeDtypeStruct((heads, length, dk), bf16),
+            jax.ShapeDtypeStruct((2 * experts_here, lanes, hidden_units), bf16),
         ),
-        in_specs=[vmem()] * 5,
-        out_specs=(vmem(),) * 3,
-        compiler_params=params(32),
-        cost_estimate=cost(2e9, 2e6),
+        in_specs=[vmem()] * 5 + [anywhere()] * 2,
+        out_specs=(vmem(),) * 4,
+        scratch_shapes=[pltpu.SemaphoreType.DMA((2,))],
+        compiler_params=params(60),
+        cost_estimate=cost(2e9, 4e6),
         name="scan",
-    )(query_proj, key_proj, value_proj, beta_logit, log_decay)
-
-    maps = [carry] + [along_x(carry, k) for k in range(1, columns)]
-    half = dk * heads // columns
-    total, before = pl.pallas_call(
+    )(
+        query_proj, key_proj, value_proj, beta_logit, log_decay,
+        expert_gate, expert_up,
+    )
+    first_weights = lax.all_gather(packed, "exp", axis=0)
+
+    maps = exchange(carry, along_x)
+    totals, before = pl.pallas_call(
         row_kernel,
         out_shape=(
-            jax.ShapeDtypeStruct((dk + half, dk), bf16),
+            jax.ShapeDtypeStruct((rows, dk + half, dk), bf16),
             jax.ShapeDtypeStruct((heads, 2 * dk, dk), bf16),
         ),
-        in_specs=[smem()] + [vmem()] * 4,
+        in_specs=[vmem()],
         out_specs=(vmem(), vmem()),
+        compiler_params=params(16),
+        cost_estimate=cost(5e7, 1e6),
         name="row",
-    )(where, *maps)
-    window = follow(along_y(total, 1), along_y(total, 2))
-    window = follow(window, along_y(window, 2))
-    arrived = along_y(window[dk:], 4)
-    quarter = (mm(arrived, window[:dk]) + window[dk:].astype(f32)).astype(bf16)
-    quarters = [quarter] + [along_x(quarter, k) for k in range(1, columns)]
+    )(maps)
+    totals = exchange(totals, along_y)
+    quarter = pl.pallas_call(
+        column_kernel,
+        out_shape=jax.ShapeDtypeStruct((columns, half, dk), bf16),
+        in_specs=[vmem()],
+        out_specs=vmem(),
+        compiler_params=params(16),
+        cost_estimate=cost(2e7, 5e5),
+        name="column",
+    )(totals)
+    quarters = exchange(quarter, along_x)
 
     gated = pl.pallas_call(
         gate_kernel,
         out_shape=jax.ShapeDtypeStruct((2, pairs, tokens, heads * dk), bf16),
-        in_specs=[smem()] + [vmem()] * 9,
+        in_specs=[vmem()] * 6,
         out_specs=vmem(),
-        scratch_shapes=[
-            pltpu.VMEM((columns, half, dk), bf16),
-            pltpu.VMEM((heads, dk, dk), bf16),
-        ],
         compiler_params=params(32),
         cost_estimate=cost(1e8, 2e6),
         name="gate",
-    )(where, *quarters, before, blend, own, output_gate, norm_gain.reshape(1, dk))
+    )(quarters, before, blend, own, output_gate, norm_gain.reshape(1, dk))
     got = pair_swap(gated[1])
-    steps = 4
-    wide = width // steps
     partial_sums = pl.pallas_call(
         project_kernel,
-        grid=(steps,),
         out_shape=jax.ShapeDtypeStruct((pairs, tokens, width), bf16),
-        in_specs=[
-            pl.BlockSpec((1, pairs, tokens, heads * dk), lambda n: (0, 0, 0, 0)),
-            pl.BlockSpec((pairs, tokens, heads * dk), lambda n: (0, 0, 0)),
-            pl.BlockSpec((heads * dk, wide), lambda n: (0, n)),
-            pl.BlockSpec((heads * dk, wide), lambda n: (0, n)),
-        ],
-        out_specs=pl.BlockSpec((pairs, tokens, wide), lambda n: (0, 0, n)),
-        compiler_params=params(32),
+        in_specs=[vmem()] * 4,
+        out_specs=vmem(),
+        compiler_params=params(24),
         cost_estimate=cost(6e8, 4e6),
         name="project",
     )(gated, got, out_weight, other_weight)
@@ -450,46 +491,44 @@
         partial_sums, "exp", 0, 0, tiled=True, axis_index_groups=same_core
     )
 
-    hidden, outgoing = pl.pallas_call(
+    hidden, outgoing, packed = pl.pallas_call(
         dispatch_kernel,
         out_shape=(
             jax.ShapeDtypeStruct((tokens, width), f32),
             jax.ShapeDtypeStruct((slots, cuts, lanes), bf16),
+            jax.ShapeDtypeStruct((experts_here, lanes, hidden_units), bf16),
         ),
-        in_specs=[smem(), vmem(), vmem(), vmem()],
-        out_specs=(vmem(), vmem()),
+        in_specs=[smem(), vmem(), vmem(), vmem(), anywhere(), vmem()],
+        out_specs=(vmem(), vmem(), anywhere()),
         scratch_shapes=[
             pltpu.VMEM((tokens * cuts, lanes), f32),
             pltpu.VMEM((tokens, cuts, lanes), bf16),
+            pltpu.SemaphoreType.DMA((experts_here * (hidden_units // lanes),)),
         ],
         compiler_params=params(32),
         cost_estimate=cost(1e6, 3e6),
         name="dispatch",
-    )(owner, parts, residual, moe_gain.reshape(1, width))
+    )(owner, parts, residual, moe_gain.reshape(1, width), expert_down, first_weights[0, 0, :16, :lanes])
+    last_weights = lax.all_gather(packed, "exp", axis=0)
     outgoing = outgoing.reshape(groups, experts_here, capacity, cuts, lanes)
     incoming = lax.all_to_all(outgoing, "ctx", 0, 0, tiled=True)
 
-    shape = (groups, 1, capacity, cuts, lanes)
-    weights = (2 * pairs, 1) + packed.shape[1:]
     answers = pl.pallas_call(
         expert_kernel,
-        grid=(experts_here,),
         out_shape=jax.ShapeDtypeStruct(incoming.shape, bf16),
-        in_specs=[
-            pl.BlockSpec(shape, lambda e: (0, e, 0, 0, 0)),
-            pl.BlockSpec(weights, lambda e: (0, e, 0, 0)),
-            pl.BlockSpec(weights, lambda e: (0, experts_here + e, 0, 0)),
-            pl.BlockSpec(weights, lambda e: (0, 2 * experts_here + e, 0, 0)),
-        ],
-        out_specs=pl.BlockSpec(shape, lambda e: (0, e, 0, 0, 0)),
+        in_specs=[vmem(), anywhere(), anywhere()],
+        out_specs=vmem(),
         scratch_shapes=[
-            pltpu.VMEM((groups * capacity * cuts, lanes), f32),
-            pltpu.VMEM((groups * capacity, width), bf16),
-        ],
+            pltpu.VMEM(first_weights.shape, bf16),
+            pltpu.VMEM(last_weights.shape, bf16),
+            pltpu.SemaphoreType.DMA((3 * experts_here,)),
+        ]
+        + [pltpu.VMEM((groups * capacity * cuts, lanes), f32)] * (2 * experts_here)
+        + [pltpu.VMEM((groups * capacity, width), bf16)] * experts_here,
         compiler_params=params(48),
         cost_estimate=cost(3e9, 16e6),
         name="experts",
-    )(incoming, gathered, gathered, gathered)
+    )(incoming, first_weights, last_weights)
     returned = lax.all_to_all(answers, "ctx", 0, 0, tiled=True).reshape(slots, cuts, lanes)
 
     return pl.pallas_call(

time: 234 us -> 210 us (0.90)
  starting transfers between devices: 63.3 us -> 24 us
  blocking collectives: 49.9 us -> 69.7 us
  other arithmetic: 2.69 us -> 0 us
  local copies, waits for them, and re-layouts: 4.84 us -> 2.19 us
    ppermute x10 -> x0, starting transfers between devices: 43.2 us -> none  [the longest x6 24.4 us: along_x(): return lax.ppermute(block, 'ctx', route)]
    all_to_all x0 -> x2, blocking collectives: none -> 24.1 us  [exchange(): lax.all_to_all(blocks, 'ctx', 0, 0, tiled=True, axis_index_groups=groups)]
    all_to_all x0 -> x1, waiting for transfers between devices: none -> 11.6 us  [exchange(): lax.all_to_all(blocks, 'ctx', 0, 0, tiled=True, axis_index_groups=groups)]
    ppermute x10 -> x0, waiting for transfers between devices: 9.3 us -> none  [the longest x6 5.83 us: along_x(): return lax.ppermute(block, 'ctx', route)]
    all_to_all x1, blocking collectives: 49.9 us -> 45.6 us  [shards(): incoming = lax.all_to_all(outgoing, 'ctx', 0, 0, tiled=True)]
    all_to_all x0 -> x1, starting transfers between devices: none -> 3.97 us  [exchange(): lax.all_to_all(blocks, 'ctx', 0, 0, tiled=True, axis_index_groups=groups)]
    pallas_call x3 -> x4, Pallas kernels: 13.1 us -> 10.9 us  [the longest x1 7.05 us: shards(): pl.pallas_call(expert_kernel, out_shape=jax.ShapeDtypeStruct(incoming.sha...]
  transfers between devices with their start and end apart: 15 -> 7, of which waited for: 8 -> 4; matrix products, arithmetic and copies ran while one was open for 1% -> 1% of each run, Pallas kernels for 6% -> 4%
where the time goes in v2:
time: 210 us; the launch traced here: 209 us
  waiting for transfers between devices  74.9 us (36%)
  blocking collectives  69.7 us (33%)
  Pallas kernels  24.6 us (12%)
  starting transfers between devices  24 us (11%)
  between operations  13.6 us (6%)
  local copies, waits for them, and re-layouts  2.19 us (1%)
    all_to_all x1, blocking collectives, shards(): incoming = lax.all_to_all(outgoing, 'ctx', 0, 0, tiled=True)  45.6 us
    all_to_all x1, waiting for transfers between devices, shards(): lax.all_to_all(answers, 'ctx', 0, 0, tiled=True).reshape(slots, cuts, lanes)  38.3 us
    all_to_all x2, blocking collectives, exchange(): lax.all_to_all(blocks, 'ctx', 0, 0, tiled=True, axis_index_groups=groups)  24.1 us
    all_to_all x1, waiting for transfers between devices, shards(): lax.all_to_all(partial_sums, 'exp', 0, 0, tiled=True, axis_index_groups=s...  23.7 us
    all_to_all x1, waiting for transfers between devices, exchange(): lax.all_to_all(blocks, 'ctx', 0, 0, tiled=True, axis_index_groups=groups)  11.6 us
    all_to_all x1, starting transfers between devices, shards(): lax.all_to_all(partial_sums, 'exp', 0, 0, tiled=True, axis_index_groups=s...  10.5 us
    pallas_call x1, Pallas kernels, shards(): pl.pallas_call(expert_kernel, out_shape=jax.ShapeDtypeStruct(incoming.sha...  7.05 us
    all_to_all x1, starting transfers between devices, shards(): lax.all_to_all(answers, 'ctx', 0, 0, tiled=True).reshape(slots, cuts, lanes)  5.58 us
  transfers between devices with their start and end apart: 7, of which 4 were waited for; matrix products, arithmetic and copies ran while one was open for 1% of the time, Pallas kernels for 4%

profile of v2, /device:TPU:2, one launch (start us, length us, event | category | flops | bytes accessed | tf_op | source)
XLA Modules:
  0.0 209.0 jit_solution(7526031796761280835)
XLA Ops:
  6.5 0.0 all-gather.5.cloned.1.call-start
  6.5 5.4 %scan.1 = (bf16[4,2,256,128]{3,2,1,0:T(8,128)(2,1)}, bf16[2,512,128]{2,1,0:T(8,128)(2,1)}, bf16[2,512,128]{2,1,0:T(8,128)(2,1)}, bf16[4,128,512]{2,1,0:T(8,128)(2,1)}) custom-call(bf16[512,128]{1,0:T(8,128)(2,1)} %q_ref.1, bf16[512,128]{1,0:T(8,128)(2,1)} %k_ref.1, bf16[512,256]{1,0:T(8,128)(2,1)} %v_ref.1, f32[2,512]{1,0:T(2,128)} %beta_ref.1, ...), custom_call_target="tpu_custom_call" | custom-call | flops 2000000000 | bytes 4000000 | tf_op jit(solution)/shard_map/scan/pallas_call | solution.py:425
  12.0 0.0 copy-start
  12.0 0.0 all-gather.5.cloned.1.call-update
  12.0 0.0 copy-start.1
  12.0 0.0 copy-start.3
  12.1 0.0 copy-start.4
  12.1 0.0 copy-start.9
  12.1 16.1 %all_to_all.30.maps_ref = bf16[4,2,256,128]{3,2,1,0:T(8,128)(2,1)S(1)} all-to-all(bf16[4,2,256,128]{3,2,1,0:T(8,128)(2,1)} %get-tuple-element.18), channel_id=1, replica_groups={{0,16,32,48},{64,80,96,112},{128,144,160,176},{192,208,224,240},{256,27..., dimensions={0} | all-to-all | bytes 1048576 | tf_op jit(solution)/shard_map/all_to_all | solution.py:409
  28.2 1.2 row.1
  29.4 4.0 %all-to-all-start.1 = ((bf16[8,192,128]{2,1,0:T(8,128)(2,1)}), bf16[8,192,128]{2,1,0:T(8,128)(2,1)S(1)}, u32[]{:S(2)}, u32[]{:S(2)}) async-start(bf16[8,192,128]{2,1,0:T(8,128)(2,1)} %get-tuple-element.19), calls=%async_computation.1 | async-start | bytes 786432 | tf_op jit(solution)/shard_map/all_to_all | solution.py:409
  33.4 0.0 copy-done
  33.4 1.9 collective-permute-start.1
  35.3 11.6 %all-to-all-done.1.totals_ref = bf16[8,192,128]{2,1,0:T(8,128)(2,1)S(1)} async-done(((bf16[8,192,128]{2,1,0:T(8,128)(2,1)}), bf16[8,192,128]{2,1,0:T(8,128)(2,1)S(1)}, u32[]{:S(2)}, u32[]{:S(2)}) %all-to-all-start.1) | async-done | bytes 393248 | tf_op jit(solution)/shard_map/all_to_all | solution.py:409
  46.9 0.8 column.1
  47.7 8.0 %all_to_all.31.quarters_ref = bf16[4,64,128]{2,1,0:T(8,128)(2,1)S(1)} all-to-all(bf16[4,64,128]{2,1,0:T(8,128)(2,1)S(1)} %column.1), channel_id=1, replica_groups={{0,16,32,48},{64,80,96,112},{128,144,160,176},{192,208,224,240},{256,27..., dimensions={0} | all-to-all | bytes 131072 | tf_op jit(solution)/shard_map/all_to_all | solution.py:409
  55.7 0.0 copy-done.1
  55.7 0.0 copy-done.3
  55.7 0.0 copy-done.4
  55.7 0.0 copy-done.9
  55.7 0.6 gate.1.kept_ref
  56.4 1.9 collective-permute-start
  58.3 0.0 collective-permute-done.1.other_ref
  58.3 1.3 collective-permute-done.got_ref
  59.6 1.8 project.1
  61.4 0.0 copy-start.10
  61.4 0.0 copy-start.2
  61.4 0.0 copy-start.5
  61.4 0.0 copy-start.6
  61.4 10.5 %all-to-all-start.3 = ((bf16[8,32,2048]{2,1,0:T(8,128)(2,1)}), bf16[8,32,2048]{2,1,0:T(8,128)(2,1)S(1)}, u32[]{:S(2)}, u32[]{:S(2)}) async-start(bf16[8,32,2048]{2,1,0:T(8,128)(2,1)} %project.1), calls=%async_computation.3 | async-start | bytes 2097152 | tf_op jit(solution)/shard_map/all_to_all | solution.py:490
  71.9 0.0 all-gather.7.cloned.1.call-start
  72.0 0.0 copy-done.10
  72.0 0.7 copy.18.ids_ref
  72.7 3.9 %route.1 = (s32[320]{0:T(512)}, s32[384]{0:T(512)}) custom-call(s32[32,10]{1,0:T(8,128)} %copy.18.ids_ref), custom_call_target="tpu_custom_call" | custom-call | tf_op jit(solution)/shard_map/route/pallas_call | solution.py:413
  76.6 0.0 all-gather.5.cloned.1.call-done
  76.6 0.7 slice_bitcast_fusion.1.after_ref
  77.3 23.7 %all-to-all-done.3.parts_ref = bf16[8,32,2048]{2,1,0:T(8,128)(2,1)S(1)} async-done(((bf16[8,32,2048]{2,1,0:T(8,128)(2,1)}), bf16[8,32,2048]{2,1,0:T(8,128)(2,1)S(1)}, u32[]{:S(2)}, u32[]{:S(2)}) %all-to-all-start.3) | async-done | bytes 1048608 | tf_op jit(solution)/shard_map/all_to_all | solution.py:490
  101.0 0.0 copy-done.2
  101.0 0.0 copy-done.5
  101.0 0.0 copy-done.6
  101.0 0.0 copy-start.8
  101.0 0.7 copy-done.8
  101.7 1.6 dispatch.1
  103.3 0.0 all-gather.7.cloned.1.call-update
  103.3 45.6 %all_to_all.32.rows_ref = bf16[32,2,6,16,128]{4,3,2,1,0:T(8,128)(2,1)S(1)} all-to-all(bf16[32,2,6,16,128]{4,3,2,1,0:T(8,128)(2,1)S(1)} %bitcast.11), channel_id=1, replica_groups=mesh['ctx'=32,'exp'=16] {'ctx'}, dimensions={0} | all-to-all | bytes 3145728 | tf_op jit(solution)/shard_map/all_to_all | solution.py:514
  148.9 0.0 all-gather.7.cloned.1.call-done
  148.9 7.0 %experts.1 = bf16[32,2,6,16,128]{4,3,2,1,0:T(8,128)(2,1)} custom-call(bf16[32,2,6,16,128]{4,3,2,1,0:T(8,128)(2,1)S(1)} %all_to_all.32.rows_ref, bf16[16,4,128,512]{3,2,1,0:T(8,128)(2,1)} %bitcast.15, bf16[16,2,128,512]{3,2,1,0:T(8,128)(2,1)} %bitcast.16), custom_call_target="tpu_custom_call" | custom-call | flops 3000000000 | bytes 16000000 | tf_op jit(solution)/shard_map/experts/pallas_call | solution.py:516
  155.9 0.0 copy-start.11
  155.9 0.0 copy-start.7
  156.0 5.6 %all-to-all-start.5 = ((bf16[32,2,6,16,128]{4,3,2,1,0:T(8,128)(2,1)}), bf16[32,2,6,16,128]{4,3,2,1,0:T(8,128)(2,1)S(1)}, u32[]{:S(2)}, u32[]{:S(2)}) async-start(bf16[32,2,6,16,128]{4,3,2,1,0:T(8,128)(2,1)} %experts.1), calls=%async_computation.5 | async-start | bytes 3145728 | tf_op jit(solution)/shard_map/all_to_all | solution.py:532
  161.5 0.0 copy-done.11
  161.6 0.1 copy.19.weight_ref
  161.6 38.3 %all-to-all-done.5 = bf16[32,2,6,16,128]{4,3,2,1,0:T(8,128)(2,1)S(1)} async-done(((bf16[32,2,6,16,128]{4,3,2,1,0:T(8,128)(2,1)}), bf16[32,2,6,16,128]{4,3,2,1,0:T(8,128)(2,1)S(1)}, u32[]{:S(2)}, u32[]{:S(2)}) %all-to-all-start.5) | async-done | bytes 1572896 | tf_op jit(solution)/shard_map/all_to_all | solution.py:532
  199.9 0.0 copy-done.7
  199.9 2.2 %combine.1 = bf16[32,2048]{1,0:T(8,128)(2,1)} custom-call(s32[320]{0:T(512)S(1)} %copy-done.7, f32[32,10]{1,0:T(8,128)S(1)} %copy.19.weight_ref, bf16[384,16,128]{2,1,0:T(8,128)(2,1)S(1)} %bitcast.10, f32[32,2048]{1,0:T(8,128)S(1)} %get-tuple-element.26.hidden_ref), custom_call_target="tpu_custom_call" | custom-call | flops 1000000 | bytes 3000000 | tf_op jit(solution)/shard_map/combine/pallas_call | solution.py:534
  (1 shorter events, 0.0 us)
Async XLA Ops:
  6.5 70.1 %all-gather.5.cloned.1.call-start = ((), (), s32[]{:S(2)}) async-start(), calls=%async_computation.6 | async-start | bytes 8912896 | tf_op jit(solution)/shard_map/all_gather | solution.py:443
  12.0 21.4 %copy-start = (bf16[256,2048]{1,0:T(8,128)(2,1)S(1)}, bf16[256,2048]{1,0:T(8,128)(2,1)}, u32[]{:S(2)}) copy-start(bf16[256,2048]{1,0:T(8,128)(2,1)} %own_ref.1) | copy-start | bytes 3145732
  12.0 43.7 %copy-start.1 = (bf16[512,256]{1,0:T(8,128)(2,1)S(1)}, bf16[512,256]{1,0:T(8,128)(2,1)}, u32[]{:S(2)}) copy-start(bf16[512,256]{1,0:T(8,128)(2,1)} %gate_ref.3) | copy-start | bytes 786436
  12.0 43.7 %copy-start.3 = (bf16[2,512,128]{2,1,0:T(8,128)(2,1)S(1)}, bf16[2,512,128]{2,1,0:T(8,128)(2,1)}, u32[]{:S(2)}) copy-start(bf16[2,512,128]{2,1,0:T(8,128)(2,1)} %get-tuple-element.21.blend_ref) | copy-start | bytes 786436
  12.1 43.7 %copy-start.4 = (bf16[2,512,128]{2,1,0:T(8,128)(2,1)S(1)}, bf16[2,512,128]{2,1,0:T(8,128)(2,1)}, u32[]{:S(2)}) copy-start(bf16[2,512,128]{2,1,0:T(8,128)(2,1)} %get-tuple-element.22.own_ref) | copy-start | bytes 786436
  12.1 43.7 %copy-start.9 = (f32[128]{0:T(128)S(1)}, f32[128]{0:T(128)}, u32[]{:S(2)}) copy-start(f32[128]{0:T(128)} %param.21) | copy-start | bytes 1540
  29.4 17.5 %all-to-all-start.1 = ((bf16[8,192,128]{2,1,0:T(8,128)(2,1)}), bf16[8,192,128]{2,1,0:T(8,128)(2,1)S(1)}, u32[]{:S(2)}, u32[]{:S(2)}) async-start(bf16[8,192,128]{2,1,0:T(8,128)(2,1)} %get-tuple-element.19), calls=%async_computation.1 | async-start | bytes 786432 | tf_op jit(solution)/shard_map/all_to_all | solution.py:409
  33.4 24.9 %collective-permute-start.1 = (bf16[256,2048]{1,0:T(8,128)(2,1)S(1)}, bf16[256,2048]{1,0:T(8,128)(2,1)S(1)}, u32[]{:S(2)}, u32[]{:S(2)}) collective-permute-start(bf16[256,2048]{1,0:T(8,128)(2,1)S(1)} %copy-done), channel_id=1, source_target_pairs={{0,1},{1,0},{2,3},{3,2},{4,5},{5,4},{6,7},{7,6},{8,9},{9,8},{10,11... | collective-permute-start | bytes 3145736 | tf_op jit(solution)/shard_map/ppermute | solution.py:406
  56.4 3.2 %collective-permute-start = (bf16[8,32,256]{2,1,0:T(8,128)(2,1)S(1)}, bf16[8,32,256]{2,1,0:T(8,128)(2,1)S(1)}, u32[]{:S(2)}, u32[]{:S(2)}) collective-permute-start(bf16[8,32,256]{2,1,0:T(8,128)(2,1)S(1)} %slice_bitcast_fusion), channel_id=1, source_target_pairs={{0,1},{1,0},{2,3},{3,2},{4,5},{5,4},{6,7},{7,6},{8,9},{9,8},{10,11... | collective-permute-start | bytes 393224 | tf_op jit(solution)/shard_map/ppermute | solution.py:406
  61.4 10.6 %copy-start.10 = (s32[32,10]{0,1:T(8,128)S(1)}, s32[32,10]{0,1:T(8,128)}, u32[]{:S(2)}) copy-start(s32[32,10]{0,1:T(8,128)} %param.25) | copy-start | bytes 3844
  61.4 39.6 %copy-start.2 = (bf16[2,512,128]{2,1,0:T(8,128)(2,1)S(1)}, bf16[2,512,128]{2,1,0:T(8,128)(2,1)}, u32[]{:S(2)}) copy-start(bf16[2,512,128]{2,1,0:T(8,128)(2,1)} %down_ref.1) | copy-start | bytes 786436
  61.4 39.6 %copy-start.5 = (bf16[32,2048]{1,0:T(8,128)(2,1)S(1)}, bf16[32,2048]{1,0:T(8,128)(2,1)}, u32[]{:S(2)}) copy-start(bf16[32,2048]{1,0:T(8,128)(2,1)} %residual_ref.1) | copy-start | bytes 393220
  61.4 39.6 %copy-start.6 = (f32[2048]{0:T(1024)S(1)}, f32[2048]{0:T(1024)}, u32[]{:S(2)}) copy-start(f32[2048]{0:T(1024)} %param.24) | copy-start | bytes 24580
  61.4 39.6 %all-to-all-start.3 = ((bf16[8,32,2048]{2,1,0:T(8,128)(2,1)}), bf16[8,32,2048]{2,1,0:T(8,128)(2,1)S(1)}, u32[]{:S(2)}, u32[]{:S(2)}) async-start(bf16[8,32,2048]{2,1,0:T(8,128)(2,1)} %project.1), calls=%async_computation.3 | async-start | bytes 2097152 | tf_op jit(solution)/shard_map/all_to_all | solution.py:490
  71.9 77.0 %all-gather.7.cloned.1.call-start = ((), (), s32[]{:S(2)}) async-start(), calls=%async_computation.7 | async-start | bytes 4456448 | tf_op jit(solution)/shard_map/all_gather | solution.py:512
  101.0 0.7 copy-start.8
  155.9 5.6 %copy-start.11 = (f32[32,10]{0,1:T(8,128)S(1)}, f32[32,10]{0,1:T(8,128)}, u32[]{:S(2)}) copy-start(f32[32,10]{0,1:T(8,128)} %param.26) | copy-start | bytes 3844
  155.9 44.0 %copy-start.7 = (s32[320]{0:T(512)S(1)}, s32[320]{0:T(512)}, u32[]{:S(2)}) copy-start(s32[320]{0:T(512)} %get-tuple-element.16.slot_ref) | copy-start | bytes 3844
  156.0 44.0 %all-to-all-start.5 = ((bf16[32,2,6,16,128]{4,3,2,1,0:T(8,128)(2,1)}), bf16[32,2,6,16,128]{4,3,2,1,0:T(8,128)(2,1)S(1)}, u32[]{:S(2)}, u32[]{:S(2)}) async-start(bf16[32,2,6,16,128]{4,3,2,1,0:T(8,128)(2,1)} %experts.1), calls=%async_computation.5 | async-start | bytes 3145728 | tf_op jit(solution)/shard_map/all_to_all | solution.py:532
Sparse Core Ops, SparseCore 0:
  12.1 64.0 all-gather.4
  103.4 39.7 all-gather.6

commit v3 on v2

--- a/solution.py
+++ b/solution.py
@@ -59,26 +59,47 @@
     return copies
 
 
-def pack_down(down_ref, packed_ref):
+def pack_moves(gate_ref, up_ref, down_ref, early_ref, late_ref):
     experts, depth, lanes = down_ref.shape
-    return [
-        (down_ref.at[e, b : b + lanes, :], packed_ref.at[e, :, b : b + lanes])
-        for e in range(experts)
-        for b in range(0, depth, lanes)
-    ]
+    rows, split = early_ref.shape[1], early_ref.shape[0]
+    halves = lanes // rows
+    moves = []
+
+    def add(source, place, *columns):
+        home = early_ref.at[place] if place < split else late_ref.at[place - split]
+        moves.append((source, home.at[(slice(None),) + columns] if columns else home))
+
+    for e in range(experts):
+        for i in range(halves):
+            part = slice(i * rows, (i + 1) * rows)
+            add(gate_ref.at[e, part], e * halves + i)
+            add(up_ref.at[e, part], (experts + e) * halves + i)
+            for b in range(0, depth, lanes):
+                add(
+                    down_ref.at[e, b + i * rows : b + (i + 1) * rows, :],
+                    (2 * experts + e) * halves + i,
+                    slice(b, b + lanes),
+                )
+    return moves
 
 
 def scan_kernel(
-    heads, q_ref, k_ref, v_ref, beta_ref, log_ref, gate_ref, up_ref,
-    carry_ref, blend_ref, own_ref, packed_ref, sems,
+    heads, q_ref, k_ref, v_ref, beta_ref, log_ref, output_gate_ref, gate_ref, up_ref, down_ref,
+    carry_ref, kept_ref, sent_ref, early_ref, late_ref, sems,
 ):
-    experts = gate_ref.shape[0]
-    copies = start_copies(
-        [(gate_ref, packed_ref.at[0:experts]), (up_ref, packed_ref.at[experts : 2 * experts])],
-        sems,
-    )
+    copies = start_copies(pack_moves(gate_ref, up_ref, down_ref, early_ref, late_ref), sems)
     length, dk = q_ref.shape
     count = length // BLOCK
+    tokens = kept_ref.shape[2]
+    first_core = lax.rem(lax.axis_index("exp"), 2) == 0
+
+    def put(part, c, lanes, value):
+        for b in range(0, BLOCK, 2 * tokens):
+            pair = (c * BLOCK + b) // (2 * tokens)
+            even, odd = value[b : b + tokens], value[b + tokens : b + 2 * tokens]
+            kept_ref[part, pair, :, lanes] = jnp.where(first_core, even, odd)
+            sent_ref[part, pair, :, lanes] = jnp.where(first_core, odd, even)
+
     row = lax.broadcasted_iota(jnp.int32, (BLOCK, BLOCK), 0)
     col = lax.broadcasted_iota(jnp.int32, (BLOCK, BLOCK), 1)
     problems = []
@@ -149,8 +170,10 @@
             state = states[h]
             low = state.astype(bf16)
             out = mm(p["queries"] - p["seen"][:, :dk], low)
-            blend_ref[h, span, :] = out[:, :dk].astype(bf16)
-            own_ref[h, span, :] = (out[:, dk:] + p["seen"][:, dk:]).astype(bf16)
+            lanes = slice(h * dk, (h + 1) * dk)
+            put(0, c, lanes, out[:, :dk].astype(bf16))
+            put(1, c, lanes, (out[:, dk:] + p["seen"][:, dk:]).astype(bf16))
+            put(2, c, lanes, output_gate_ref[span, lanes])
             push = p["push"]
             moved = mm(push[:, :dk], low)
             states[h] = jnp.concatenate(
@@ -210,7 +233,7 @@
 
 def column_kernel(totals_ref, out_ref):
     dk = totals_ref.shape[2]
-    y = lax.axis_index("ctx") // out_ref.shape[0]
+    y = lax.axis_index("ctx") // (out_ref.shape[0] // 2)
 
     state = jnp.zeros(out_ref.shape[1:], f32)
     for j in range(totals_ref.shape[0] - 1):
@@ -221,33 +244,35 @@
         out_ref[place] = state
 
 
-def gate_kernel(
-    quarters_ref, before_ref, blend_ref, own_ref, gate_ref, gain_ref, out_ref
+def project_kernel(
+    quarters_ref, before_ref, other_before_ref, kept_ref, got_ref, gain_ref, weight_ref,
+    other_weight_ref, out_ref,
 ):
     core = lax.rem(lax.axis_index("exp"), 2)
-    heads, length, dk = own_ref.shape
-    pairs, tokens = out_ref.shape[1], out_ref.shape[2]
-    share = quarters_ref.shape[0] // heads
+    heads, _, dk = before_ref.shape
+    _, pairs, tokens, _ = kept_ref.shape
+    rows = pairs * tokens
+    columns = quarters_ref.shape[0] // 2
+    share = columns // heads
     gain = gain_ref[...]
-    for h in range(heads):
-        row_state = jnp.concatenate([quarters_ref[share * h + i] for i in range(share)], 0)
-        entry = mm(row_state, before_ref[h, :dk, :]) + before_ref[h, dk:, :].astype(f32)
-        mixed = own_ref[h].astype(f32) + mm_nt(blend_ref[h], entry)
-        scale = lax.rsqrt(jnp.mean(mixed * mixed, 1, keepdims=True) + 1e-06)
-        gates = gate_ref[:, h * dk : (h + 1) * dk].astype(f32)
-        gated = (mixed * scale * gain * (gates * sigmoid(gates))).astype(bf16)
-        for parity in range(2):
-            mine = lax.rem(parity + core, 2)
-            for pair in range(pairs):
-                start = (2 * pair + parity) * tokens
-                out_ref[mine, pair, :, h * dk : (h + 1) * dk] = gated[start : start + tokens]
-
-
-def project_kernel(kept_ref, got_ref, own_ref, other_ref, out_ref):
-    pairs, tokens, width = got_ref.shape
-    rows = pairs * tokens
-    total = mm(kept_ref[0].reshape(rows, width), own_ref[...])
-    total = total + mm(got_ref[...].reshape(rows, width), other_ref[...])
+    total = 0.0
+    for source, before, base, weight in (
+        (kept_ref, before_ref, core * columns, weight_ref),
+        (got_ref, other_before_ref, (1 - core) * columns, other_weight_ref),
+    ):
+        gated = []
+        for h in range(heads):
+            lanes = slice(h * dk, (h + 1) * dk)
+            row_state = jnp.concatenate(
+                [quarters_ref[base + share * h + i] for i in range(share)], 0
+            )
+            entry = mm(row_state, before[h, :dk, :]) + before[h, dk:, :].astype(f32)
+            mixed = mm_nt(source[0, :, :, lanes].reshape(rows, dk), entry)
+            mixed = mixed + source[1, :, :, lanes].astype(f32).reshape(rows, dk)
+            scale = lax.rsqrt(jnp.mean(mixed * mixed, 1, keepdims=True) + 1e-06)
+            gates = source[2, :, :, lanes].astype(f32).reshape(rows, dk)
+            gated.append((mixed * scale * gain * (gates * sigmoid(gates))).astype(bf16))
+        total = total + mm(jnp.concatenate(gated, 1), weight[...])
     out_ref[...] = total.astype(bf16).reshape(out_ref.shape)
 
 
@@ -277,10 +302,9 @@
 
 
 def dispatch_kernel(
-    owner_ref, parts_ref, residual_ref, gain_ref, down_ref, after_ref,
-    hidden_ref, out_ref, packed_ref, rows_ref, tiles_ref, sems,
+    owner_ref, parts_ref, residual_ref, gain_ref, after_ref, late_ref,
+    hidden_ref, out_ref, same_late_ref, rows_ref, tiles_ref,
 ):
-    copies = start_copies(pack_down(down_ref, packed_ref), sems)
     sources, tokens, width = parts_ref.shape
     lanes = out_ref.shape[2]
     cuts = width // lanes
@@ -303,20 +327,33 @@
         return carry
 
     lax.fori_loop(0, out_ref.shape[0] // unroll, place, 0)
-    for copy in copies:
-        copy.wait()
-
-
-def expert_kernel(rows_ref, first_ref, last_ref, out_ref, first_vmem, last_vmem, sems, *scratch):
+
+
+def expert_kernel(rows_ref, early_ref, late_ref, out_ref, weights, sems, *scratch):
     groups, experts, capacity, cuts, lanes = rows_ref.shape
-    moves = []
-    for e in range(experts):
-        moves.append((first_ref.at[:, e], first_vmem.at[:, e]))
-        moves.append((first_ref.at[:, experts + e], first_vmem.at[:, experts + e]))
-        moves.append((last_ref.at[:, e], last_vmem.at[:, e]))
-    copies = start_copies(moves, sems)
+    split, height = early_ref.shape[1:3]
+    halves = lanes // height
+    order = [
+        (m * experts + e) * halves + i for e in range(experts) for m in range(3) for i in range(halves)
+    ]
+    copies = start_copies(
+        [
+            (
+                early_ref.at[:, m] if m < split else late_ref.at[:, m - split],
+                weights.at[:, m],
+            )
+            for m in order
+        ],
+        sems,
+    )
+
+    def matrix(e, m):
+        for i in range(halves):
+            copies[(3 * e + m) * halves + i].wait()
+        return slice((m * experts + e) * halves, (m * experts + e + 1) * halves)
+
     rows = groups * capacity
-    hidden_units = first_ref.shape[3]
+    hidden_units = early_ref.shape[3]
     depth = cuts * lanes
     wide_in, wide_out, flat = scratch[:experts], scratch[experts : 2 * experts], scratch[2 * experts :]
     for e in range(experts):
@@ -326,19 +363,17 @@
             flat[e][:, j * lanes : (j + 1) * lanes] = part.astype(bf16)
     for e in range(experts):
         tokens = flat[e][...]
-        copies[3 * e].wait()
-        first = mm(tokens, first_vmem[:, e].reshape(depth, hidden_units))
-        copies[3 * e + 1].wait()
-        second = mm(tokens, first_vmem[:, experts + e].reshape(depth, hidden_units))
+        first = mm(tokens, weights[:, matrix(e, 0)].reshape(depth, hidden_units))
+        second = mm(tokens, weights[:, matrix(e, 1)].reshape(depth, hidden_units))
         inner = (first * sigmoid(first) * second).astype(bf16)
-        copies[3 * e + 2].wait()
+        last = matrix(e, 2)
         for j in range(0, cuts, 2):
             columns = []
             for k in (j, j + 1):
                 columns.append(
                     jnp.concatenate(
                         [
-                            last_vmem[k, e, :, b : b + lanes]
+                            weights[k, last, :, b : b + lanes].reshape(lanes, lanes)
                             for b in range(0, hidden_units, lanes)
                         ],
                         0,
@@ -422,25 +457,31 @@
         name="route",
     )(expert_ids)
 
-    carry, blend, own, packed = pl.pallas_call(
+    early_halves = 7
+    package = jax.ShapeDtypeStruct((3, pairs, tokens, heads * dk), bf16)
+    carry, kept, sent, early, late = pl.pallas_call(
         functools.partial(scan_kernel, heads),
         out_shape=(
             jax.ShapeDtypeStruct((columns, heads, 2 * dk, dk), bf16),
-            jax.ShapeDtypeStruct((heads, length, dk), bf16),
-            jax.ShapeDtypeStruct((heads, length, dk), bf16),
-            jax.ShapeDtypeStruct((2 * experts_here, lanes, hidden_units), bf16),
+            package,
+            package,
+            jax.ShapeDtypeStruct((early_halves, lanes // 2, hidden_units), bf16),
+            jax.ShapeDtypeStruct((6 * experts_here - early_halves, lanes // 2, hidden_units), bf16),
         ),
-        in_specs=[vmem()] * 5 + [anywhere()] * 2,
-        out_specs=(vmem(),) * 4,
-        scratch_shapes=[pltpu.SemaphoreType.DMA((2,))],
+        in_specs=[vmem()] * 6 + [anywhere()] * 3,
+        out_specs=(vmem(),) * 5,
+        scratch_shapes=[
+            pltpu.SemaphoreType.DMA((2 * experts_here * (2 + hidden_units // lanes),))
+        ],
         compiler_params=params(60),
         cost_estimate=cost(2e9, 4e6),
         name="scan",
     )(
-        query_proj, key_proj, value_proj, beta_logit, log_decay,
-        expert_gate, expert_up,
-    )
-    first_weights = lax.all_gather(packed, "exp", axis=0)
+        query_proj, key_proj, value_proj, beta_logit, log_decay, output_gate,
+        expert_gate, expert_up, expert_down,
+    )
+    got = pair_swap(sent)
+    early = lax.all_gather(early, "exp", axis=0)
 
     maps = exchange(carry, along_x)
     totals, before = pl.pallas_call(
@@ -455,61 +496,66 @@
         cost_estimate=cost(5e7, 1e6),
         name="row",
     )(maps)
+    other_before = pair_swap(before)
     totals = exchange(totals, along_y)
     quarter = pl.pallas_call(
         column_kernel,
-        out_shape=jax.ShapeDtypeStruct((columns, half, dk), bf16),
+        out_shape=jax.ShapeDtypeStruct((2 * columns, half, dk), bf16),
         in_specs=[vmem()],
         out_specs=vmem(),
         compiler_params=params(16),
         cost_estimate=cost(2e7, 5e5),
         name="column",
     )(totals)
-    quarters = exchange(quarter, along_x)
-
-    gated = pl.pallas_call(
-        gate_kernel,
-        out_shape=jax.ShapeDtypeStruct((2, pairs, tokens, heads * dk), bf16),
-        in_specs=[vmem()] * 6,
-        out_specs=vmem(),
-        compiler_params=params(32),
-        cost_estimate=cost(1e8, 2e6),
-        name="gate",
-    )(quarters, before, blend, own, output_gate, norm_gain.reshape(1, dk))
-    got = pair_swap(gated[1])
+    quarters = lax.all_to_all(
+        quarter,
+        ("ctx", "exp"),
+        0,
+        0,
+        tiled=True,
+        axis_index_groups=[
+            [(y * columns + x) * 2 * pairs + 2 * z + c for c in range(2) for x in range(columns)]
+            for y in range(rows)
+            for z in range(pairs)
+        ],
+    )
+
     partial_sums = pl.pallas_call(
         project_kernel,
         out_shape=jax.ShapeDtypeStruct((pairs, tokens, width), bf16),
-        in_specs=[vmem()] * 4,
+        in_specs=[vmem()] * 8,
         out_specs=vmem(),
         compiler_params=params(24),
         cost_estimate=cost(6e8, 4e6),
         name="project",
-    )(gated, got, out_weight, other_weight)
+    )(
+        quarters, before, other_before, kept, got, norm_gain.reshape(1, dk),
+        out_weight, other_weight,
+    )
     same_core = [[c + 2 * z for z in range(pairs)] for c in range(2)]
     parts = lax.all_to_all(
         partial_sums, "exp", 0, 0, tiled=True, axis_index_groups=same_core
     )
 
-    hidden, outgoing, packed = pl.pallas_call(
+    hidden, outgoing, late = pl.pallas_call(
         dispatch_kernel,
         out_shape=(
             jax.ShapeDtypeStruct((tokens, width), f32),
             jax.ShapeDtypeStruct((slots, cuts, lanes), bf16),
-            jax.ShapeDtypeStruct((experts_here, lanes, hidden_units), bf16),
+            jax.ShapeDtypeStruct(late.shape, bf16),
         ),
-        in_specs=[smem(), vmem(), vmem(), vmem(), anywhere(), vmem()],
+        in_specs=[smem(), vmem(), vmem(), vmem(), vmem(), anywhere()],
         out_specs=(vmem(), vmem(), anywhere()),
+        input_output_aliases={5: 2},
         scratch_shapes=[
             pltpu.VMEM((tokens * cuts, lanes), f32),
             pltpu.VMEM((tokens, cuts, lanes), bf16),
-            pltpu.SemaphoreType.DMA((experts_here * (hidden_units // lanes),)),
         ],
         compiler_params=params(32),
         cost_estimate=cost(1e6, 3e6),
         name="dispatch",
-    )(owner, parts, residual, moe_gain.reshape(1, width), expert_down, first_weights[0, 0, :16, :lanes])
-    last_weights = lax.all_gather(packed, "exp", axis=0)
+    )(owner, parts, residual, moe_gain.reshape(1, width), early[0, 0, :16, :lanes], late)
+    late = lax.all_gather(late, "exp", axis=0)
     outgoing = outgoing.reshape(groups, experts_here, capacity, cuts, lanes)
     incoming = lax.all_to_all(outgoing, "ctx", 0, 0, tiled=True)
 
@@ -519,16 +565,15 @@
         in_specs=[vmem(), anywhere(), anywhere()],
         out_specs=vmem(),
         scratch_shapes=[
-            pltpu.VMEM(first_weights.shape, bf16),
-            pltpu.VMEM(last_weights.shape, bf16),
-            pltpu.SemaphoreType.DMA((3 * experts_here,)),
+            pltpu.VMEM((2 * pairs, 6 * experts_here, lanes // 2, hidden_units), bf16),
+            pltpu.SemaphoreType.DMA((6 * experts_here,)),
         ]
         + [pltpu.VMEM((groups * capacity * cuts, lanes), f32)] * (2 * experts_here)
         + [pltpu.VMEM((groups * capacity, width), bf16)] * experts_here,
         compiler_params=params(48),
         cost_estimate=cost(3e9, 16e6),
         name="experts",
-    )(incoming, first_weights, last_weights)
+    )(incoming, early, late)
     returned = lax.all_to_all(answers, "ctx", 0, 0, tiled=True).reshape(slots, cuts, lanes)
 
     return pl.pallas_call(

time: 210 us -> 207 us (0.986)
  blocking collectives: 69.7 us -> 43.8 us
  starting transfers between devices: 24 us -> 40.5 us
  waiting for transfers between devices: 74.9 us -> 80.8 us
    all_to_all x2 -> x0, blocking collectives: 24.1 us -> none  [exchange(): lax.all_to_all(blocks, 'ctx', 0, 0, tiled=True, axis_index_groups=groups)]
    all_to_all x1 -> x2, starting transfers between devices: 3.97 us -> 13.5 us  [exchange(): lax.all_to_all(blocks, 'ctx', 0, 0, tiled=True, axis_index_groups=groups)]
    all_to_all x0 -> x1, starting transfers between devices: none -> 4.74 us  [shards(): lax.all_to_all(quarter, ('ctx', 'exp'), 0, 0, tiled=True, axis_index_grou...]
    all_to_all x0 -> x1, waiting for transfers between devices: none -> 4.5 us  [shards(): lax.all_to_all(quarter, ('ctx', 'exp'), 0, 0, tiled=True, axis_index_grou...]
    ppermute x2 -> x3, starting transfers between devices: 3.84 us -> 6.22 us  [pair_swap(): return lax.ppermute(block, 'exp', [(i, i ^ 1) for i in range(2 * pairs)])]
    all_to_all x1 -> x2, waiting for transfers between devices: 11.6 us -> 13.6 us  [exchange(): lax.all_to_all(blocks, 'ctx', 0, 0, tiled=True, axis_index_groups=groups)]
  transfers between devices with their start and end apart: 7 -> 10, of which waited for: 4 -> 5; matrix products, arithmetic and copies ran while one was open for 1% -> 1% of each run, Pallas kernels for 4% -> 4%
where the time goes in v3:
time: 207 us
  waiting for transfers between devices  80.8 us (39%)
  blocking collectives  43.8 us (21%)
  starting transfers between devices  40.5 us (20%)
  Pallas kernels  25.7 us (12%)
  between operations  13.5 us (7%)
  local copies, waits for them, and re-layouts  2.17 us (1%)
    all_to_all x1, blocking collectives, shards(): incoming = lax.all_to_all(outgoing, 'ctx', 0, 0, tiled=True)  43.8 us
    all_to_all x1, waiting for transfers between devices, shards(): lax.all_to_all(answers, 'ctx', 0, 0, tiled=True).reshape(slots, cuts, lanes)  38.7 us
    all_to_all x1, waiting for transfers between devices, shards(): lax.all_to_all(partial_sums, 'exp', 0, 0, tiled=True, axis_index_groups=s...  24 us
    all_to_all x2, waiting for transfers between devices, exchange(): lax.all_to_all(blocks, 'ctx', 0, 0, tiled=True, axis_index_groups=groups)  13.6 us
    all_to_all x2, starting transfers between devices, exchange(): lax.all_to_all(blocks, 'ctx', 0, 0, tiled=True, axis_index_groups=groups)  13.5 us
    all_to_all x1, starting transfers between devices, shards(): lax.all_to_all(partial_sums, 'exp', 0, 0, tiled=True, axis_index_groups=s...  10.5 us
    pallas_call x1, Pallas kernels, shards(): pl.pallas_call(expert_kernel, out_shape=jax.ShapeDtypeStruct(incoming.sha...  7.05 us
    ppermute x3, starting transfers between devices, pair_swap(): return lax.ppermute(block, 'exp', [(i, i ^ 1) for i in range(2 * pairs)])  6.22 us
  transfers between devices with their start and end apart: 10, of which 5 were waited for; matrix products, arithmetic and copies ran while one was open for 1% of the time, Pallas kernels for 4%

profile of v3, /device:TPU:2, one launch (start us, length us, event | category | flops | bytes accessed | tf_op | source)
XLA Modules:
  0.0 206.6 jit_solution(6816769230915845889)
XLA Ops:
  6.5 0.0 copy-start
  6.5 0.0 all-gather.5.cloned.1.call-start
  6.5 6.0 %scan.1 = (bf16[4,2,256,128]{3,2,1,0:T(8,128)(2,1)}, bf16[3,8,32,256]{3,2,1,0:T(8,128)(2,1)}, bf16[3,8,32,256]{3,2,1,0:T(8,128)(2,1)}, bf16[7,64,512]{2,1,0:T(8,128)(2,1)}, bf16[5,64,512]{2,1,0:T(8,128)(2,1)}) custom-call(bf16[512,128]{1,0:T(8,128)(2,1)} %q_ref.1, bf16[512,128]{1,0:T(8,128)(2,1)} %k_ref.1, bf16[512,256]{1,0:T(8,128)(2,1)} %v_ref.1, ...), custom_call_target="tpu_custom_call" | custom-call | flops 2000000000 | bytes 4000000 | tf_op jit(solution)/shard_map/scan/pallas_call | solution.py:462
  12.6 0.0 all-gather.5.cloned.1.call-update
  12.6 0.0 copy-start.1
  12.6 0.0 copy-start.6
  12.6 9.5 %all-to-all-start = ((bf16[4,2,256,128]{3,2,1,0:T(8,128)(2,1)}), bf16[4,2,256,128]{3,2,1,0:T(8,128)(2,1)S(1)}, u32[]{:S(2)}, u32[]{:S(2)}) async-start(bf16[4,2,256,128]{3,2,1,0:T(8,128)(2,1)} %get-tuple-element.19), calls=%async_computation | async-start | bytes 1048576 | tf_op jit(solution)/shard_map/all_to_all | solution.py:444
  22.1 0.0 copy-done
  22.1 1.9 collective-permute-start.2
  24.0 4.7 %all-to-all-done.maps_ref = bf16[4,2,256,128]{3,2,1,0:T(8,128)(2,1)S(1)} async-done(((bf16[4,2,256,128]{3,2,1,0:T(8,128)(2,1)}), bf16[4,2,256,128]{3,2,1,0:T(8,128)(2,1)S(1)}, u32[]{:S(2)}, u32[]{:S(2)}) %all-to-all-start) | async-done | bytes 524320 | tf_op jit(solution)/shard_map/all_to_all | solution.py:444
  28.7 1.2 row.1
  29.9 4.0 %all-to-all-start.1 = ((bf16[8,192,128]{2,1,0:T(8,128)(2,1)}), bf16[8,192,128]{2,1,0:T(8,128)(2,1)S(1)}, u32[]{:S(2)}, u32[]{:S(2)}) async-start(bf16[8,192,128]{2,1,0:T(8,128)(2,1)} %get-tuple-element.20), calls=%async_computation.1 | async-start | bytes 786432 | tf_op jit(solution)/shard_map/all_to_all | solution.py:444
  33.9 1.9 collective-permute-start.1
  35.8 2.4 %collective-permute-start = (bf16[2,256,128]{2,1,0:T(8,128)(2,1)S(1)}, bf16[2,256,128]{2,1,0:T(8,128)(2,1)S(1)}, u32[]{:S(2)}, u32[]{:S(2)}) collective-permute-start(bf16[2,256,128]{2,1,0:T(8,128)(2,1)S(1)} %get-tuple-element.21.before_ref), channel_id=1, source_target_pairs={{0,1},{1,0},{2,3},{3,2},{4,5},{5,4},{6,7},{7,6},{8,9},{9,8},{10,11... | collective-permute-start | bytes 393224 | tf_op jit(solution)/shard_map/ppermute | solution.py:441
  38.2 8.9 %all-to-all-done.1.totals_ref = bf16[8,192,128]{2,1,0:T(8,128)(2,1)S(1)} async-done(((bf16[8,192,128]{2,1,0:T(8,128)(2,1)}), bf16[8,192,128]{2,1,0:T(8,128)(2,1)S(1)}, u32[]{:S(2)}, u32[]{:S(2)}) %all-to-all-start.1) | async-done | bytes 393248 | tf_op jit(solution)/shard_map/all_to_all | solution.py:444
  47.1 1.5 column.1
  48.6 4.7 %all-to-all-start.2 = ((bf16[8,64,128]{2,1,0:T(8,128)(2,1)}), bf16[8,64,128]{2,1,0:T(8,128)(2,1)S(1)}, u32[]{:S(2)}, u32[]{:S(2)}) async-start(bf16[8,64,128]{2,1,0:T(8,128)(2,1)} %column.1), calls=%async_computation.2 | async-start | bytes 262144 | tf_op jit(solution)/shard_map/all_to_all | solution.py:510
  53.3 0.0 collective-permute-done.1.got_ref
  53.3 0.0 collective-permute-done.other_before_ref
  53.3 0.0 collective-permute-done.2.other_weight_ref
  53.3 4.5 %all-to-all-done.2.quarters_ref = bf16[8,64,128]{2,1,0:T(8,128)(2,1)S(1)} async-done(((bf16[8,64,128]{2,1,0:T(8,128)(2,1)}), bf16[8,64,128]{2,1,0:T(8,128)(2,1)S(1)}, u32[]{:S(2)}, u32[]{:S(2)}) %all-to-all-start.2) | async-done | bytes 131104 | tf_op jit(solution)/shard_map/all_to_all | solution.py:510
  57.8 0.0 copy-done.1
  57.8 0.0 copy-done.6
  57.8 2.4 %project.1 = bf16[8,32,2048]{2,1,0:T(8,128)(2,1)} custom-call(bf16[8,64,128]{2,1,0:T(8,128)(2,1)S(1)} %all-to-all-done.2.quarters_ref, bf16[2,256,128]{2,1,0:T(8,128)(2,1)S(1)} %get-tuple-element.21.before_ref, bf16[2,256,128]{2,1,0:T(8,128)(2,1)S(1)} %collective-permute-done.other_before_ref, bf16[3,8,32,256]{3,2,1,0:T(8,128)(2,1)S(1)} %copy-done.1, ...), custom_call_target="tpu_custom_call" | custom-call | flops 600000000 | bytes 4000000 | tf_op jit(solution)/shard_map/project/pallas_call | solution.py:523
  60.2 0.0 copy-start.7
  60.2 0.0 copy-start.2
  60.2 0.0 copy-start.3
  60.2 10.5 %all-to-all-start.3 = ((bf16[8,32,2048]{2,1,0:T(8,128)(2,1)}), bf16[8,32,2048]{2,1,0:T(8,128)(2,1)S(1)}, u32[]{:S(2)}, u32[]{:S(2)}) async-start(bf16[8,32,2048]{2,1,0:T(8,128)(2,1)} %project.1), calls=%async_computation.3 | async-start | bytes 2097152 | tf_op jit(solution)/shard_map/all_to_all | solution.py:536
  70.7 0.0 all-gather.7.cloned.1.call-start
  70.7 0.0 copy-done.7
  70.7 0.7 copy.19.ids_ref
  71.4 3.9 %route.1 = (s32[320]{0:T(512)}, s32[384]{0:T(512)}) custom-call(s32[32,10]{1,0:T(8,128)} %copy.19.ids_ref), custom_call_target="tpu_custom_call" | custom-call | tf_op jit(solution)/shard_map/route/pallas_call | solution.py:448
  75.4 0.0 all-gather.5.cloned.1.call-done
  75.4 0.7 slice_bitcast_fusion.after_ref
  76.1 24.0 %all-to-all-done.3.parts_ref = bf16[8,32,2048]{2,1,0:T(8,128)(2,1)S(1)} async-done(((bf16[8,32,2048]{2,1,0:T(8,128)(2,1)}), bf16[8,32,2048]{2,1,0:T(8,128)(2,1)S(1)}, u32[]{:S(2)}, u32[]{:S(2)}) %all-to-all-start.3) | async-done | bytes 1048608 | tf_op jit(solution)/shard_map/all_to_all | solution.py:536
  100.1 0.0 copy-done.2
  100.1 0.0 copy-done.3
  100.1 0.0 copy-start.5
  100.1 0.7 copy-done.5
  100.7 1.5 dispatch.1
  102.2 0.0 all-gather.7.cloned.1.call-update
  102.3 43.8 %all_to_all.30.rows_ref = bf16[32,2,6,16,128]{4,3,2,1,0:T(8,128)(2,1)S(1)} all-to-all(bf16[32,2,6,16,128]{4,3,2,1,0:T(8,128)(2,1)S(1)} %bitcast.9), channel_id=1, replica_groups=mesh['ctx'=32,'exp'=16] {'ctx'}, dimensions={0} | all-to-all | bytes 3145728 | tf_op jit(solution)/shard_map/all_to_all | solution.py:560
  146.0 0.0 all-gather.7.cloned.1.call-done
  146.0 7.1 %experts.1 = bf16[32,2,6,16,128]{4,3,2,1,0:T(8,128)(2,1)} custom-call(bf16[32,2,6,16,128]{4,3,2,1,0:T(8,128)(2,1)S(1)} %all_to_all.30.rows_ref, bf16[16,7,64,512]{3,2,1,0:T(8,128)(2,1)} %bitcast.13, bf16[16,5,64,512]{3,2,1,0:T(8,128)(2,1)} %bitcast.14), custom_call_target="tpu_custom_call" | custom-call | flops 3000000000 | bytes 16000000 | tf_op jit(solution)/shard_map/experts/pallas_call | solution.py:562
  153.1 0.0 copy-start.8
  153.1 0.0 copy-start.4
  153.1 5.6 %all-to-all-start.5 = ((bf16[32,2,6,16,128]{4,3,2,1,0:T(8,128)(2,1)}), bf16[32,2,6,16,128]{4,3,2,1,0:T(8,128)(2,1)S(1)}, u32[]{:S(2)}, u32[]{:S(2)}) async-start(bf16[32,2,6,16,128]{4,3,2,1,0:T(8,128)(2,1)} %experts.1), calls=%async_computation.5 | async-start | bytes 3145728 | tf_op jit(solution)/shard_map/all_to_all | solution.py:577
  158.7 0.0 copy-done.8
  158.7 0.1 copy.20.weight_ref
  158.8 38.7 %all-to-all-done.5 = bf16[32,2,6,16,128]{4,3,2,1,0:T(8,128)(2,1)S(1)} async-done(((bf16[32,2,6,16,128]{4,3,2,1,0:T(8,128)(2,1)}), bf16[32,2,6,16,128]{4,3,2,1,0:T(8,128)(2,1)S(1)}, u32[]{:S(2)}, u32[]{:S(2)}) %all-to-all-start.5) | async-done | bytes 1572896 | tf_op jit(solution)/shard_map/all_to_all | solution.py:577
  197.5 0.0 copy-done.4
  197.5 2.2 %combine.1 = bf16[32,2048]{1,0:T(8,128)(2,1)} custom-call(s32[320]{0:T(512)S(1)} %copy-done.4, f32[32,10]{1,0:T(8,128)S(1)} %copy.20.weight_ref, bf16[384,16,128]{2,1,0:T(8,128)(2,1)S(1)} %bitcast.8, f32[32,2048]{1,0:T(8,128)S(1)} %get-tuple-element.28.hidden_ref), custom_call_target="tpu_custom_call" | custom-call | flops 1000000 | bytes 3000000 | tf_op jit(solution)/shard_map/combine/pallas_call | solution.py:579
Async XLA Ops:
  6.5 15.6 %copy-start = (bf16[256,2048]{1,0:T(8,128)(2,1)S(1)}, bf16[256,2048]{1,0:T(8,128)(2,1)}, u32[]{:S(2)}) copy-start(bf16[256,2048]{1,0:T(8,128)(2,1)} %weight_ref.2) | copy-start | bytes 3145732
  6.5 68.9 %all-gather.5.cloned.1.call-start = ((), (), s32[]{:S(2)}) async-start(), calls=%async_computation.6 | async-start | bytes 7798784 | tf_op jit(solution)/shard_map/all_gather | solution.py:484
  12.6 45.2 %copy-start.1 = (bf16[3,8,32,256]{3,2,1,0:T(8,128)(2,1)S(1)}, bf16[3,8,32,256]{3,2,1,0:T(8,128)(2,1)}, u32[]{:S(2)}) copy-start(bf16[3,8,32,256]{3,2,1,0:T(8,128)(2,1)} %get-tuple-element.22.kept_ref) | copy-start | bytes 1179652
  12.6 45.2 %copy-start.6 = (f32[128]{0:T(128)S(1)}, f32[128]{0:T(128)}, u32[]{:S(2)}) copy-start(f32[128]{0:T(128)} %param.21) | copy-start | bytes 1540
  12.6 16.1 %all-to-all-start = ((bf16[4,2,256,128]{3,2,1,0:T(8,128)(2,1)}), bf16[4,2,256,128]{3,2,1,0:T(8,128)(2,1)S(1)}, u32[]{:S(2)}, u32[]{:S(2)}) async-start(bf16[4,2,256,128]{3,2,1,0:T(8,128)(2,1)} %get-tuple-element.19), calls=%async_computation | async-start | bytes 1048576 | tf_op jit(solution)/shard_map/all_to_all | solution.py:444
  22.1 31.2 %collective-permute-start.2 = (bf16[256,2048]{1,0:T(8,128)(2,1)S(1)}, bf16[256,2048]{1,0:T(8,128)(2,1)S(1)}, u32[]{:S(2)}, u32[]{:S(2)}) collective-permute-start(bf16[256,2048]{1,0:T(8,128)(2,1)S(1)} %copy-done), channel_id=1, source_target_pairs={{0,1},{1,0},{2,3},{3,2},{4,5},{5,4},{6,7},{7,6},{8,9},{9,8},{10,11... | collective-permute-start | bytes 3145736 | tf_op jit(solution)/shard_map/ppermute | solution.py:441
  29.9 17.2 %all-to-all-start.1 = ((bf16[8,192,128]{2,1,0:T(8,128)(2,1)}), bf16[8,192,128]{2,1,0:T(8,128)(2,1)S(1)}, u32[]{:S(2)}, u32[]{:S(2)}) async-start(bf16[8,192,128]{2,1,0:T(8,128)(2,1)} %get-tuple-element.20), calls=%async_computation.1 | async-start | bytes 786432 | tf_op jit(solution)/shard_map/all_to_all | solution.py:444
  33.9 19.5 %collective-permute-start.1 = (bf16[3,8,32,256]{3,2,1,0:T(8,128)(2,1)}, bf16[3,8,32,256]{3,2,1,0:T(8,128)(2,1)S(1)}, u32[]{:S(2)}, u32[]{:S(2)}) collective-permute-start(bf16[3,8,32,256]{3,2,1,0:T(8,128)(2,1)} %get-tuple-element.23), channel_id=1, source_target_pairs={{0,1},{1,0},{2,3},{3,2},{4,5},{5,4},{6,7},{7,6},{8,9},{9,8},{10,11... | collective-permute-start | bytes 1179656 | tf_op jit(solution)/shard_map/ppermute | solution.py:441
  35.8 17.5 %collective-permute-start = (bf16[2,256,128]{2,1,0:T(8,128)(2,1)S(1)}, bf16[2,256,128]{2,1,0:T(8,128)(2,1)S(1)}, u32[]{:S(2)}, u32[]{:S(2)}) collective-permute-start(bf16[2,256,128]{2,1,0:T(8,128)(2,1)S(1)} %get-tuple-element.21.before_ref), channel_id=1, source_target_pairs={{0,1},{1,0},{2,3},{3,2},{4,5},{5,4},{6,7},{7,6},{8,9},{9,8},{10,11... | collective-permute-start | bytes 393224 | tf_op jit(solution)/shard_map/ppermute | solution.py:441
  48.6 9.3 %all-to-all-start.2 = ((bf16[8,64,128]{2,1,0:T(8,128)(2,1)}), bf16[8,64,128]{2,1,0:T(8,128)(2,1)S(1)}, u32[]{:S(2)}, u32[]{:S(2)}) async-start(bf16[8,64,128]{2,1,0:T(8,128)(2,1)} %column.1), calls=%async_computation.2 | async-start | bytes 262144 | tf_op jit(solution)/shard_map/all_to_all | solution.py:510
  60.2 10.5 %copy-start.7 = (s32[32,10]{0,1:T(8,128)S(1)}, s32[32,10]{0,1:T(8,128)}, u32[]{:S(2)}) copy-start(s32[32,10]{0,1:T(8,128)} %param.25) | copy-start | bytes 3844
  60.2 39.8 %copy-start.2 = (bf16[32,2048]{1,0:T(8,128)(2,1)S(1)}, bf16[32,2048]{1,0:T(8,128)(2,1)}, u32[]{:S(2)}) copy-start(bf16[32,2048]{1,0:T(8,128)(2,1)} %residual_ref.1) | copy-start | bytes 393220
  60.2 39.8 %copy-start.3 = (f32[2048]{0:T(1024)S(1)}, f32[2048]{0:T(1024)}, u32[]{:S(2)}) copy-start(f32[2048]{0:T(1024)} %param.24) | copy-start | bytes 24580
  60.2 39.8 %all-to-all-start.3 = ((bf16[8,32,2048]{2,1,0:T(8,128)(2,1)}), bf16[8,32,2048]{2,1,0:T(8,128)(2,1)S(1)}, u32[]{:S(2)}, u32[]{:S(2)}) async-start(bf16[8,32,2048]{2,1,0:T(8,128)(2,1)} %project.1), calls=%async_computation.3 | async-start | bytes 2097152 | tf_op jit(solution)/shard_map/all_to_all | solution.py:536
  70.7 75.3 %all-gather.7.cloned.1.call-start = ((), (), s32[]{:S(2)}) async-start(), calls=%async_computation.7 | async-start | bytes 5570560 | tf_op jit(solution)/shard_map/all_gather | solution.py:558
  100.1 0.7 copy-start.5
  153.1 5.6 %copy-start.8 = (f32[32,10]{0,1:T(8,128)S(1)}, f32[32,10]{0,1:T(8,128)}, u32[]{:S(2)}) copy-start(f32[32,10]{0,1:T(8,128)} %param.26) | copy-start | bytes 3844
  153.1 44.4 %copy-start.4 = (s32[320]{0:T(512)S(1)}, s32[320]{0:T(512)}, u32[]{:S(2)}) copy-start(s32[320]{0:T(512)} %get-tuple-element.17.slot_ref) | copy-start | bytes 3844
  153.1 44.4 %all-to-all-start.5 = ((bf16[32,2,6,16,128]{4,3,2,1,0:T(8,128)(2,1)}), bf16[32,2,6,16,128]{4,3,2,1,0:T(8,128)(2,1)S(1)}, u32[]{:S(2)}, u32[]{:S(2)}) async-start(bf16[32,2,6,16,128]{4,3,2,1,0:T(8,128)(2,1)} %experts.1), calls=%async_computation.5 | async-start | bytes 3145728 | tf_op jit(solution)/shard_map/all_to_all | solution.py:577
Sparse Core Ops, SparseCore 0:
  12.7 59.0 all-gather.4
  102.4 38.3 all-gather.6

commit v4 on v3

--- a/solution.py
+++ b/solution.py
@@ -329,7 +329,7 @@
     lax.fori_loop(0, out_ref.shape[0] // unroll, place, 0)
 
 
-def expert_kernel(rows_ref, early_ref, late_ref, out_ref, weights, sems, *scratch):
+def expert_kernel(rows_ref, early_ref, late_ref, out_ref, weights, ready, sems, out_sems, *scratch):
     groups, experts, capacity, cuts, lanes = rows_ref.shape
     split, height = early_ref.shape[1:3]
     halves = lanes // height
@@ -356,6 +356,7 @@
     hidden_units = early_ref.shape[3]
     depth = cuts * lanes
     wide_in, wide_out, flat = scratch[:experts], scratch[experts : 2 * experts], scratch[2 * experts :]
+    sent = []
     for e in range(experts):
         wide_in[e][...] = rows_ref[:, e].astype(f32).reshape(rows * cuts, lanes)
         for j in range(cuts):
@@ -382,7 +383,11 @@
             answer = mm(inner, jnp.concatenate(columns, 1))
             wide_out[e][pl.ds(j, rows, stride=cuts), :] = answer[:, :lanes]
             wide_out[e][pl.ds(j + 1, rows, stride=cuts), :] = answer[:, lanes:]
-        out_ref[:, e] = wide_out[e][...].astype(bf16).reshape(groups, capacity, cuts, lanes)
+        ready[e] = wide_out[e][...].astype(bf16).reshape(groups, capacity, cuts, lanes)
+        sent.append(pltpu.make_async_copy(ready.at[e], out_ref.at[:, e], out_sems.at[e]))
+        sent[e].start()
+    for copy in sent:
+        copy.wait()
 
 
 def combine_kernel(topk, slot_ref, weight_ref, back_ref, hidden_ref, out_ref, total):
@@ -396,7 +401,7 @@
         total[pl.ds(pl.multiple_of(t * cuts, cuts), cuts), :] = acc
         return carry
 
-    lax.fori_loop(0, tokens, add, 0, unroll=2)
+    lax.fori_loop(0, tokens, add, 0, unroll=4)
     for j in range(cuts):
         span = slice(j * lanes, (j + 1) * lanes)
         mixture = total[pl.ds(j, tokens, stride=cuts), :]
@@ -563,10 +568,12 @@
         expert_kernel,
         out_shape=jax.ShapeDtypeStruct(incoming.shape, bf16),
         in_specs=[vmem(), anywhere(), anywhere()],
-        out_specs=vmem(),
+        out_specs=anywhere(),
         scratch_shapes=[
             pltpu.VMEM((2 * pairs, 6 * experts_here, lanes // 2, hidden_units), bf16),
+            pltpu.VMEM((experts_here, groups, capacity, cuts, lanes), bf16),
             pltpu.SemaphoreType.DMA((6 * experts_here,)),
+            pltpu.SemaphoreType.DMA((experts_here,)),
         ]
         + [pltpu.VMEM((groups * capacity * cuts, lanes), f32)] * (2 * experts_here)
         + [pltpu.VMEM((groups * capacity, width), bf16)] * experts_here,

time: 207 us -> 207 us (level)
  no operation moved by 1% of the time
where the time goes in v4:
time: 207 us; the launch traced here: 206 us
  waiting for transfers between devices  80.8 us (39%)
  blocking collectives  43.8 us (21%)
  starting transfers between devices  40.5 us (20%)
  Pallas kernels  25.5 us (12%)
  between operations  13.5 us (7%)
  local copies, waits for them, and re-layouts  2.17 us (1%)
    all_to_all x1, blocking collectives, shards(): incoming = lax.all_to_all(outgoing, 'ctx', 0, 0, tiled=True)  43.8 us
    all_to_all x1, waiting for transfers between devices, shards(): lax.all_to_all(answers, 'ctx', 0, 0, tiled=True).reshape(slots, cuts, lanes)  38.7 us
    all_to_all x1, waiting for transfers between devices, shards(): lax.all_to_all(partial_sums, 'exp', 0, 0, tiled=True, axis_index_groups=s...  24 us
    all_to_all x2, waiting for transfers between devices, exchange(): lax.all_to_all(blocks, 'ctx', 0, 0, tiled=True, axis_index_groups=groups)  13.6 us
    all_to_all x2, starting transfers between devices, exchange(): lax.all_to_all(blocks, 'ctx', 0, 0, tiled=True, axis_index_groups=groups)  13.5 us
    all_to_all x1, starting transfers between devices, shards(): lax.all_to_all(partial_sums, 'exp', 0, 0, tiled=True, axis_index_groups=s...  10.5 us
    pallas_call x1, Pallas kernels, shards(): pl.pallas_call(expert_kernel, out_shape=jax.ShapeDtypeStruct(incoming.sha...  6.82 us
    ppermute x3, starting transfers between devices, pair_swap(): return lax.ppermute(block, 'exp', [(i, i ^ 1) for i in range(2 * pairs)])  6.22 us
  transfers between devices with their start and end apart: 10, of which 5 were waited for; matrix products, arithmetic and copies ran while one was open for 1% of the time, Pallas kernels for 4%

profile of v4, /device:TPU:2, one launch (start us, length us, event | category | flops | bytes accessed | tf_op | source)
XLA Modules:
  0.0 206.3 jit_solution(8578138776493570805)
XLA Ops:
  6.5 0.0 copy-start
  6.5 0.0 all-gather.5.cloned.1.call-start
  6.5 6.0 %scan.1 = (bf16[4,2,256,128]{3,2,1,0:T(8,128)(2,1)}, bf16[3,8,32,256]{3,2,1,0:T(8,128)(2,1)}, bf16[3,8,32,256]{3,2,1,0:T(8,128)(2,1)}, bf16[7,64,512]{2,1,0:T(8,128)(2,1)}, bf16[5,64,512]{2,1,0:T(8,128)(2,1)}) custom-call(bf16[512,128]{1,0:T(8,128)(2,1)} %q_ref.1, bf16[512,128]{1,0:T(8,128)(2,1)} %k_ref.1, bf16[512,256]{1,0:T(8,128)(2,1)} %v_ref.1, ...), custom_call_target="tpu_custom_call" | custom-call | flops 2000000000 | bytes 4000000 | tf_op jit(solution)/shard_map/scan/pallas_call | solution.py:467
  12.6 0.0 all-gather.5.cloned.1.call-update
  12.6 0.0 copy-start.1
  12.6 0.0 copy-start.6
  12.6 9.5 %all-to-all-start = ((bf16[4,2,256,128]{3,2,1,0:T(8,128)(2,1)}), bf16[4,2,256,128]{3,2,1,0:T(8,128)(2,1)S(1)}, u32[]{:S(2)}, u32[]{:S(2)}) async-start(bf16[4,2,256,128]{3,2,1,0:T(8,128)(2,1)} %get-tuple-element.19), calls=%async_computation | async-start | bytes 1048576 | tf_op jit(solution)/shard_map/all_to_all | solution.py:449
  22.1 0.0 copy-done
  22.1 1.9 collective-permute-start.2
  24.0 4.7 %all-to-all-done.maps_ref = bf16[4,2,256,128]{3,2,1,0:T(8,128)(2,1)S(1)} async-done(((bf16[4,2,256,128]{3,2,1,0:T(8,128)(2,1)}), bf16[4,2,256,128]{3,2,1,0:T(8,128)(2,1)S(1)}, u32[]{:S(2)}, u32[]{:S(2)}) %all-to-all-start) | async-done | bytes 524320 | tf_op jit(solution)/shard_map/all_to_all | solution.py:449
  28.7 1.2 row.1
  29.9 4.0 %all-to-all-start.1 = ((bf16[8,192,128]{2,1,0:T(8,128)(2,1)}), bf16[8,192,128]{2,1,0:T(8,128)(2,1)S(1)}, u32[]{:S(2)}, u32[]{:S(2)}) async-start(bf16[8,192,128]{2,1,0:T(8,128)(2,1)} %get-tuple-element.20), calls=%async_computation.1 | async-start | bytes 786432 | tf_op jit(solution)/shard_map/all_to_all | solution.py:449
  33.9 1.9 collective-permute-start.1
  35.8 2.4 %collective-permute-start = (bf16[2,256,128]{2,1,0:T(8,128)(2,1)S(1)}, bf16[2,256,128]{2,1,0:T(8,128)(2,1)S(1)}, u32[]{:S(2)}, u32[]{:S(2)}) collective-permute-start(bf16[2,256,128]{2,1,0:T(8,128)(2,1)S(1)} %get-tuple-element.21.before_ref), channel_id=1, source_target_pairs={{0,1},{1,0},{2,3},{3,2},{4,5},{5,4},{6,7},{7,6},{8,9},{9,8},{10,11... | collective-permute-start | bytes 393224 | tf_op jit(solution)/shard_map/ppermute | solution.py:446
  38.2 8.9 %all-to-all-done.1.totals_ref = bf16[8,192,128]{2,1,0:T(8,128)(2,1)S(1)} async-done(((bf16[8,192,128]{2,1,0:T(8,128)(2,1)}), bf16[8,192,128]{2,1,0:T(8,128)(2,1)S(1)}, u32[]{:S(2)}, u32[]{:S(2)}) %all-to-all-start.1) | async-done | bytes 393248 | tf_op jit(solution)/shard_map/all_to_all | solution.py:449
  47.1 1.5 column.1
  48.6 4.7 %all-to-all-start.2 = ((bf16[8,64,128]{2,1,0:T(8,128)(2,1)}), bf16[8,64,128]{2,1,0:T(8,128)(2,1)S(1)}, u32[]{:S(2)}, u32[]{:S(2)}) async-start(bf16[8,64,128]{2,1,0:T(8,128)(2,1)} %column.1), calls=%async_computation.2 | async-start | bytes 262144 | tf_op jit(solution)/shard_map/all_to_all | solution.py:515
  53.3 0.0 collective-permute-done.1.got_ref
  53.3 0.0 collective-permute-done.other_before_ref
  53.3 0.0 collective-permute-done.2.other_weight_ref
  53.3 4.5 %all-to-all-done.2.quarters_ref = bf16[8,64,128]{2,1,0:T(8,128)(2,1)S(1)} async-done(((bf16[8,64,128]{2,1,0:T(8,128)(2,1)}), bf16[8,64,128]{2,1,0:T(8,128)(2,1)S(1)}, u32[]{:S(2)}, u32[]{:S(2)}) %all-to-all-start.2) | async-done | bytes 131104 | tf_op jit(solution)/shard_map/all_to_all | solution.py:515
  57.8 0.0 copy-done.1
  57.8 0.0 copy-done.6
  57.8 2.4 %project.1 = bf16[8,32,2048]{2,1,0:T(8,128)(2,1)} custom-call(bf16[8,64,128]{2,1,0:T(8,128)(2,1)S(1)} %all-to-all-done.2.quarters_ref, bf16[2,256,128]{2,1,0:T(8,128)(2,1)S(1)} %get-tuple-element.21.before_ref, bf16[2,256,128]{2,1,0:T(8,128)(2,1)S(1)} %collective-permute-done.other_before_ref, bf16[3,8,32,256]{3,2,1,0:T(8,128)(2,1)S(1)} %copy-done.1, ...), custom_call_target="tpu_custom_call" | custom-call | flops 600000000 | bytes 4000000 | tf_op jit(solution)/shard_map/project/pallas_call | solution.py:528
  60.2 0.0 copy-start.7
  60.2 0.0 copy-start.2
  60.2 0.0 copy-start.3
  60.2 10.5 %all-to-all-start.3 = ((bf16[8,32,2048]{2,1,0:T(8,128)(2,1)}), bf16[8,32,2048]{2,1,0:T(8,128)(2,1)S(1)}, u32[]{:S(2)}, u32[]{:S(2)}) async-start(bf16[8,32,2048]{2,1,0:T(8,128)(2,1)} %project.1), calls=%async_computation.3 | async-start | bytes 2097152 | tf_op jit(solution)/shard_map/all_to_all | solution.py:541
  70.7 0.0 all-gather.7.cloned.1.call-start
  70.7 0.0 copy-done.7
  70.7 0.7 copy.19.ids_ref
  71.4 3.9 %route.1 = (s32[320]{0:T(512)}, s32[384]{0:T(512)}) custom-call(s32[32,10]{1,0:T(8,128)} %copy.19.ids_ref), custom_call_target="tpu_custom_call" | custom-call | tf_op jit(solution)/shard_map/route/pallas_call | solution.py:453
  75.4 0.0 all-gather.5.cloned.1.call-done
  75.4 0.7 slice_bitcast_fusion.after_ref
  76.1 24.0 %all-to-all-done.3.parts_ref = bf16[8,32,2048]{2,1,0:T(8,128)(2,1)S(1)} async-done(((bf16[8,32,2048]{2,1,0:T(8,128)(2,1)}), bf16[8,32,2048]{2,1,0:T(8,128)(2,1)S(1)}, u32[]{:S(2)}, u32[]{:S(2)}) %all-to-all-start.3) | async-done | bytes 1048608 | tf_op jit(solution)/shard_map/all_to_all | solution.py:541
  100.1 0.0 copy-done.2
  100.1 0.0 copy-done.3
  100.1 0.0 copy-start.5
  100.1 0.7 copy-done.5
  100.7 1.5 dispatch.1
  102.2 0.0 all-gather.7.cloned.1.call-update
  102.3 43.8 %all_to_all.30.rows_ref = bf16[32,2,6,16,128]{4,3,2,1,0:T(8,128)(2,1)S(1)} all-to-all(bf16[32,2,6,16,128]{4,3,2,1,0:T(8,128)(2,1)S(1)} %bitcast.9), channel_id=1, replica_groups=mesh['ctx'=32,'exp'=16] {'ctx'}, dimensions={0} | all-to-all | bytes 3145728 | tf_op jit(solution)/shard_map/all_to_all | solution.py:565
  146.0 0.0 all-gather.7.cloned.1.call-done
  146.0 6.8 %experts.1 = bf16[32,2,6,16,128]{4,3,2,1,0:T(8,128)(2,1)} custom-call(bf16[32,2,6,16,128]{4,3,2,1,0:T(8,128)(2,1)S(1)} %all_to_all.30.rows_ref, bf16[16,7,64,512]{3,2,1,0:T(8,128)(2,1)} %bitcast.13, bf16[16,5,64,512]{3,2,1,0:T(8,128)(2,1)} %bitcast.14), custom_call_target="tpu_custom_call" | custom-call | flops 3000000000 | bytes 16000000 | tf_op jit(solution)/shard_map/experts/pallas_call | solution.py:567
  152.9 0.0 copy-start.8
  152.9 0.0 copy-start.4
  152.9 5.6 %all-to-all-start.5 = ((bf16[32,2,6,16,128]{4,3,2,1,0:T(8,128)(2,1)}), bf16[32,2,6,16,128]{4,3,2,1,0:T(8,128)(2,1)S(1)}, u32[]{:S(2)}, u32[]{:S(2)}) async-start(bf16[32,2,6,16,128]{4,3,2,1,0:T(8,128)(2,1)} %experts.1), calls=%async_computation.5 | async-start | bytes 3145728 | tf_op jit(solution)/shard_map/all_to_all | solution.py:584
  158.5 0.0 copy-done.8
  158.5 0.1 copy.20.weight_ref
  158.6 38.7 %all-to-all-done.5 = bf16[32,2,6,16,128]{4,3,2,1,0:T(8,128)(2,1)S(1)} async-done(((bf16[32,2,6,16,128]{4,3,2,1,0:T(8,128)(2,1)}), bf16[32,2,6,16,128]{4,3,2,1,0:T(8,128)(2,1)S(1)}, u32[]{:S(2)}, u32[]{:S(2)}) %all-to-all-start.5) | async-done | bytes 1572896 | tf_op jit(solution)/shard_map/all_to_all | solution.py:584
  197.3 0.0 copy-done.4
  197.3 2.1 %combine.1 = bf16[32,2048]{1,0:T(8,128)(2,1)} custom-call(s32[320]{0:T(512)S(1)} %copy-done.4, f32[32,10]{1,0:T(8,128)S(1)} %copy.20.weight_ref, bf16[384,16,128]{2,1,0:T(8,128)(2,1)S(1)} %bitcast.8, f32[32,2048]{1,0:T(8,128)S(1)} %get-tuple-element.28.hidden_ref), custom_call_target="tpu_custom_call" | custom-call | flops 1000000 | bytes 3000000 | tf_op jit(solution)/shard_map/combine/pallas_call | solution.py:586
Async XLA Ops:
  6.5 15.6 %copy-start = (bf16[256,2048]{1,0:T(8,128)(2,1)S(1)}, bf16[256,2048]{1,0:T(8,128)(2,1)}, u32[]{:S(2)}) copy-start(bf16[256,2048]{1,0:T(8,128)(2,1)} %weight_ref.2) | copy-start | bytes 3145732
  6.5 68.9 %all-gather.5.cloned.1.call-start = ((), (), s32[]{:S(2)}) async-start(), calls=%async_computation.6 | async-start | bytes 7798784 | tf_op jit(solution)/shard_map/all_gather | solution.py:489
  12.6 45.2 %copy-start.1 = (bf16[3,8,32,256]{3,2,1,0:T(8,128)(2,1)S(1)}, bf16[3,8,32,256]{3,2,1,0:T(8,128)(2,1)}, u32[]{:S(2)}) copy-start(bf16[3,8,32,256]{3,2,1,0:T(8,128)(2,1)} %get-tuple-element.22.kept_ref) | copy-start | bytes 1179652
  12.6 45.2 %copy-start.6 = (f32[128]{0:T(128)S(1)}, f32[128]{0:T(128)}, u32[]{:S(2)}) copy-start(f32[128]{0:T(128)} %param.21) | copy-start | bytes 1540
  12.6 16.1 %all-to-all-start = ((bf16[4,2,256,128]{3,2,1,0:T(8,128)(2,1)}), bf16[4,2,256,128]{3,2,1,0:T(8,128)(2,1)S(1)}, u32[]{:S(2)}, u32[]{:S(2)}) async-start(bf16[4,2,256,128]{3,2,1,0:T(8,128)(2,1)} %get-tuple-element.19), calls=%async_computation | async-start | bytes 1048576 | tf_op jit(solution)/shard_map/all_to_all | solution.py:449
  22.1 31.2 %collective-permute-start.2 = (bf16[256,2048]{1,0:T(8,128)(2,1)S(1)}, bf16[256,2048]{1,0:T(8,128)(2,1)S(1)}, u32[]{:S(2)}, u32[]{:S(2)}) collective-permute-start(bf16[256,2048]{1,0:T(8,128)(2,1)S(1)} %copy-done), channel_id=1, source_target_pairs={{0,1},{1,0},{2,3},{3,2},{4,5},{5,4},{6,7},{7,6},{8,9},{9,8},{10,11... | collective-permute-start | bytes 3145736 | tf_op jit(solution)/shard_map/ppermute | solution.py:446
  29.9 17.2 %all-to-all-start.1 = ((bf16[8,192,128]{2,1,0:T(8,128)(2,1)}), bf16[8,192,128]{2,1,0:T(8,128)(2,1)S(1)}, u32[]{:S(2)}, u32[]{:S(2)}) async-start(bf16[8,192,128]{2,1,0:T(8,128)(2,1)} %get-tuple-element.20), calls=%async_computation.1 | async-start | bytes 786432 | tf_op jit(solution)/shard_map/all_to_all | solution.py:449
  33.9 19.5 %collective-permute-start.1 = (bf16[3,8,32,256]{3,2,1,0:T(8,128)(2,1)}, bf16[3,8,32,256]{3,2,1,0:T(8,128)(2,1)S(1)}, u32[]{:S(2)}, u32[]{:S(2)}) collective-permute-start(bf16[3,8,32,256]{3,2,1,0:T(8,128)(2,1)} %get-tuple-element.23), channel_id=1, source_target_pairs={{0,1},{1,0},{2,3},{3,2},{4,5},{5,4},{6,7},{7,6},{8,9},{9,8},{10,11... | collective-permute-start | bytes 1179656 | tf_op jit(solution)/shard_map/ppermute | solution.py:446
  35.8 17.5 %collective-permute-start = (bf16[2,256,128]{2,1,0:T(8,128)(2,1)S(1)}, bf16[2,256,128]{2,1,0:T(8,128)(2,1)S(1)}, u32[]{:S(2)}, u32[]{:S(2)}) collective-permute-start(bf16[2,256,128]{2,1,0:T(8,128)(2,1)S(1)} %get-tuple-element.21.before_ref), channel_id=1, source_target_pairs={{0,1},{1,0},{2,3},{3,2},{4,5},{5,4},{6,7},{7,6},{8,9},{9,8},{10,11... | collective-permute-start | bytes 393224 | tf_op jit(solution)/shard_map/ppermute | solution.py:446
  48.6 9.3 %all-to-all-start.2 = ((bf16[8,64,128]{2,1,0:T(8,128)(2,1)}), bf16[8,64,128]{2,1,0:T(8,128)(2,1)S(1)}, u32[]{:S(2)}, u32[]{:S(2)}) async-start(bf16[8,64,128]{2,1,0:T(8,128)(2,1)} %column.1), calls=%async_computation.2 | async-start | bytes 262144 | tf_op jit(solution)/shard_map/all_to_all | solution.py:515
  60.2 10.5 %copy-start.7 = (s32[32,10]{0,1:T(8,128)S(1)}, s32[32,10]{0,1:T(8,128)}, u32[]{:S(2)}) copy-start(s32[32,10]{0,1:T(8,128)} %param.25) | copy-start | bytes 3844
  60.2 39.8 %copy-start.2 = (bf16[32,2048]{1,0:T(8,128)(2,1)S(1)}, bf16[32,2048]{1,0:T(8,128)(2,1)}, u32[]{:S(2)}) copy-start(bf16[32,2048]{1,0:T(8,128)(2,1)} %residual_ref.1) | copy-start | bytes 393220
  60.2 39.8 %copy-start.3 = (f32[2048]{0:T(1024)S(1)}, f32[2048]{0:T(1024)}, u32[]{:S(2)}) copy-start(f32[2048]{0:T(1024)} %param.24) | copy-start | bytes 24580
  60.2 39.8 %all-to-all-start.3 = ((bf16[8,32,2048]{2,1,0:T(8,128)(2,1)}), bf16[8,32,2048]{2,1,0:T(8,128)(2,1)S(1)}, u32[]{:S(2)}, u32[]{:S(2)}) async-start(bf16[8,32,2048]{2,1,0:T(8,128)(2,1)} %project.1), calls=%async_computation.3 | async-start | bytes 2097152 | tf_op jit(solution)/shard_map/all_to_all | solution.py:541
  70.7 75.3 %all-gather.7.cloned.1.call-start = ((), (), s32[]{:S(2)}) async-start(), calls=%async_computation.7 | async-start | bytes 5570560 | tf_op jit(solution)/shard_map/all_gather | solution.py:563
  100.1 0.7 copy-start.5
  152.9 5.6 %copy-start.8 = (f32[32,10]{0,1:T(8,128)S(1)}, f32[32,10]{0,1:T(8,128)}, u32[]{:S(2)}) copy-start(f32[32,10]{0,1:T(8,128)} %param.26) | copy-start | bytes 3844
  152.9 44.4 %copy-start.4 = (s32[320]{0:T(512)S(1)}, s32[320]{0:T(512)}, u32[]{:S(2)}) copy-start(s32[320]{0:T(512)} %get-tuple-element.17.slot_ref) | copy-start | bytes 3844
  152.9 44.4 %all-to-all-start.5 = ((bf16[32,2,6,16,128]{4,3,2,1,0:T(8,128)(2,1)}), bf16[32,2,6,16,128]{4,3,2,1,0:T(8,128)(2,1)S(1)}, u32[]{:S(2)}, u32[]{:S(2)}) async-start(bf16[32,2,6,16,128]{4,3,2,1,0:T(8,128)(2,1)} %experts.1), calls=%async_computation.5 | async-start | bytes 3145728 | tf_op jit(solution)/shard_map/all_to_all | solution.py:584
Sparse Core Ops, SparseCore 0:
  12.7 59.0 all-gather.4
  102.4 38.3 all-gather.6
